TPU v7x, 128 devices: a whole 4x4x4 slice. The times are simulated.
128 devices in a mesh: space: 32 (over z, x, core), mode: 4 (over y).
Axes of the slice: x: 4, y: 4, z: 4, core: 2. Of those that a mesh axis runs over, the one named last changes fastest.
Arguments:
- probe: float32 [8, 2, 2048, 4096], P('mode', None, 'space'), may hold values from -6 to 6
- specimen: bfloat16 [2, 2, 2048, 4096], P(None, None, 'space', 'mode'), may hold values from -4 to 4
- kernels: float32 [2, 2, 24], replicated, may hold values from -0.9 to 0.9
Outputs:
- exit_wave: float32 [8, 2, 2048, 4096], P('mode', None, 'space')
All inputs are finite; a program needn't handle non-finite values.
Results may differ from a plain program's by a relative error of at most 0.0003.
Values may be sent and summed in bfloat16 or wider, within the bound.
No kernel may reach another device: no remote copies, remote signals or barrier semaphores. Data moves between devices by JAX's collectives and lax.ppermute only.
A program may use at most 64 MiB of HBM per device.

v0:
```python
import functools

import jax
import jax.numpy as jnp
from jax import lax
from jax.experimental import pallas as pl
from jax.experimental.pallas import tpu as pltpu
from jax.sharding import PartitionSpec as P

TAPS = 24
HALF = TAPS // 2
LANES = 128
OUTER = 24
INNER = 16
PIECES = 4
MODE, ODD, UP, DOWN = range(4)
CHUNK = 512
GROUP = 4
f32 = jnp.float32
bf16 = jnp.bfloat16
VMEM = pl.BlockSpec(memory_space=pltpu.VMEM)
SMEM = pl.BlockSpec(memory_space=pltpu.SMEM)
HBM = pl.BlockSpec(memory_space=pltpu.HBM)


def in_hbm(x):
    return pltpu.with_memory_space_constraint(x, pltpu.HBM)


def in_vmem(x):
    return pltpu.with_memory_space_constraint(x, pltpu.VMEM)


def split(x):
    high = x.astype(bf16)
    return high, (x - high.astype(f32)).astype(bf16)


def look_up(tap, kernels, axis):
    real = jnp.zeros(tap.shape, f32)
    imag = jnp.zeros(tap.shape, f32)
    for t in range(TAPS):
        here = tap == t
        real = jnp.where(here, kernels[axis, 0, t], real)
        imag = jnp.where(here, kernels[axis, 1, t], imag)
    return real, imag


def position(index, own, edge):
    outer = index >= 2 * own
    line = jnp.where(outer, index - 2 * own, index)
    size = jnp.where(outer, 2 * edge, own)
    imag = line >= size
    line = jnp.where(imag, line - size, line)
    return jnp.where(outer, jnp.where(line < edge, line - edge, line - edge + own), line), imag


def row_band(kernels, own, out_edge, in_edge):
    shape = (2 * own + 4 * out_edge, 2 * own + 4 * in_edge)
    to, to_imag = position(lax.broadcasted_iota(jnp.int32, shape, 0), own, out_edge)
    at, at_imag = position(lax.broadcasted_iota(jnp.int32, shape, 1), own, in_edge)
    real, imag = look_up(at - to + HALF, kernels, 0)
    return split(jnp.where(to_imag == at_imag, real, jnp.where(to_imag, imag, -imag)))


def column_rows(source, is_imag, kernels):
    j = lax.broadcasted_iota(jnp.int32, source.shape, 1)
    real, imag = look_up(source - j + HALF, kernels, 1)
    left = jnp.where(is_imag, -imag, real)
    right = jnp.where(is_imag, real, imag)
    return split(left), split(right)


def tail_source(lane):
    is_imag = (lane >= 32) & (lane < 96)
    plain = jnp.where(is_imag, lane ^ 64, lane)
    source = jnp.where(plain < 64, plain + LANES, plain - LANES)
    inside = (plain < HALF) | (plain >= LANES - HALF)
    return jnp.where(inside, source, 1 << 20), is_imag


def edges_kernel(for_odd, place, probe, out, held, sems):
    odd = place[ODD]
    row = (odd if for_odd else 1 - odd) * (probe.shape[2] - OUTER)
    rows = pl.ds(pl.multiple_of(row, 8), OUTER)
    steps = [(m, p) for m in range(probe.shape[0]) for p in range(2)]
    takes = [pltpu.make_async_copy(probe.at[m, p, rows], held.at[m, p], sems.at[0, m, p]) for m, p in steps]
    gives = [pltpu.make_async_copy(held.at[m, p], out.at[m, p], sems.at[1, m, p]) for m, p in steps]
    for take in takes:
        take.start()
    for take, give in zip(takes, gives):
        take.wait()
        give.start()
    for give in gives:
        give.wait()


def edges(for_odd, place, probe):
    shape = (*probe.shape[:2], OUTER, probe.shape[3])
    return pl.pallas_call(
        functools.partial(edges_kernel, for_odd),
        out_shape=jax.ShapeDtypeStruct(shape, f32),
        in_specs=[SMEM, HBM],
        out_specs=HBM,
        scratch_shapes=[pltpu.VMEM(shape, f32), pltpu.SemaphoreType.DMA((2, shape[0], 2))],
        compiler_params=pltpu.CompilerParams(vmem_limit_bytes=4 * 1024 * 1024),
        name="edges_cross" if for_odd else "edges_inner",
    )(place, in_hbm(probe))


def prepare_kernel(kernels, row0h, row0l, row1h, row1l, col):
    own = row1h.shape[0] // 2
    row0h[...], row0l[...] = row_band(kernels, own, INNER, OUTER)
    row1h[...], row1l[...] = row_band(kernels, own, 0, INNER)
    lane = lax.broadcasted_iota(jnp.int32, (LANES, LANES), 0)
    for plane in range(2):
        left, right = column_rows(lane, jnp.full(lane.shape, plane == 1), kernels)
        for group, part in ((0, 0), (1, 0), (2, 1)):
            at = pl.ds((2 * group + plane) * LANES, LANES)
            col[at, :LANES] = left[part]
            col[at, LANES:] = right[part]
    source, is_imag = tail_source(lane)
    left, right = column_rows(source, is_imag, kernels)
    col[6 * LANES : 7 * LANES, :LANES] = left[0]
    col[6 * LANES : 7 * LANES, LANES:] = right[0]
    moved = (lane + LANES - 32) & (LANES - 1)
    source_moved, imag_moved = tail_source(moved)
    left_moved, right_moved = column_rows(source_moved, imag_moved, kernels)
    here = source < (1 << 19)
    col[7 * LANES :, :LANES] = jnp.where(here, left[0].astype(f32), left_moved[1].astype(f32)).astype(bf16)
    col[7 * LANES :, LANES:] = jnp.where(here, right[0].astype(f32), right_moved[1].astype(f32)).astype(bf16)


def prepare(kernels, own):
    mid = 2 * own + 4 * INNER
    shapes = [(mid, 2 * own + 4 * OUTER)] * 2 + [(2 * own, mid)] * 2 + [(8 * LANES, 2 * LANES)]
    return pl.pallas_call(
        prepare_kernel,
        out_shape=[pltpu.VMEM(s, bf16) for s in shapes],
        in_specs=[SMEM],
        out_specs=[VMEM] * 5,
        compiler_params=pltpu.CompilerParams(vmem_limit_bytes=8 * 1024 * 1024),
        name="prepare",
    )(kernels)


def dot(a, b):
    return jnp.dot(a, b, preferred_element_type=f32)


def row_stage(x_high, x_low, band_high, band_low):
    n = band_high.shape[0]
    both = dot(jnp.concatenate([band_high[...], band_low[...]], axis=0), x_high)
    return both[:n] + both[n:] + dot(band_high[...], x_low)


def product(f_real, f_imag, t_real, t_imag):
    return f_real * t_real - f_imag * t_imag, f_real * t_imag + f_imag * t_real


def lanes(block):
    return slice(block * LANES, (block + 1) * LANES)


def block_rows(j, rows, n=1):
    return slice(j * rows, (j + n) * rows)


def put(blocks, j, planes):
    rows, width = planes[0].shape
    for p, plane in enumerate(planes):
        high, low = split(plane)
        for b in range(width // LANES):
            at = block_rows(j + b, rows)
            blocks[at, lanes(p)] = high[:, lanes(b)]
            blocks[at, lanes(p + 2)] = low[:, lanes(b)]


def joined(place, piece):
    return jnp.where(lax.rem(place[MODE] + piece + PIECES - 1, PIECES) == PIECES - 1, 0.0, 1.0)


def column_stage(place, blocks, tails, col, js, rows, emit):
    total = blocks.shape[0] // rows
    per = total // PIECES
    lane = lax.broadcasted_iota(jnp.int16, (rows, LANES), 1)
    plain = lane & 63
    middle = (lane >= 32) & (lane < 96)
    used = (plain < HALF) | (plain >= 64 - HALF)

    def beside(j, step, k):
        x = blocks[block_rows((j + step) % total, rows), lanes(k)]
        if (j + (step > 0)) % per:
            return x
        keep = joined(place, (j // per - (step < 0)) % PIECES)
        return (x.astype(f32) * keep).astype(bf16)

    for n, j in enumerate(js):
        side = [jnp.where(lane < 64, beside(j, 1, k), beside(j, -1, k)) for k in range(4)]
        high = jnp.where(middle, pltpu.roll(side[1], 64, 1), side[0])
        low = jnp.where(middle, pltpu.roll(side[3], 64, 1), side[2])
        tails[block_rows(n, rows), lanes(0)] = high
        tails[block_rows(n, rows), lanes(1)] = jnp.where(used, low, pltpu.roll(high, 32, 1))
    two = 2 * LANES
    done = 0
    while done < len(js):
        first = js[done] % total
        n = min(len(js) - done, total - first, GROUP)
        at = block_rows(first, rows, n)
        main = blocks[at, :two]
        result = dot(main, col[:two, :]) + dot(blocks[at, two:], col[two : 2 * two, :])
        result = result + dot(main, col[2 * two : 3 * two, :]) + dot(tails[block_rows(done, rows, n), :], col[3 * two :, :])
        for b in range(n):
            part = result[block_rows(b, rows)]
            emit(first + b, part[:, :LANES], part[:, LANES:])
        done += n


def chunks(width):
    return [slice(c, c + CHUNK) for c in range(0, width, CHUNK)]


def keep_columns(lines, rows):
    def emit(j, real, imag):
        for p, plane in enumerate((real, imag)):
            for k, part in enumerate(split(plane)):
                lines[k, p * rows : (p + 1) * rows, lanes(j)] = part

    return emit


def piece_columns(place, q, piece):
    return pl.ds(pl.multiple_of(lax.rem(place[MODE] + q + PIECES - 1, PIECES) * piece, piece), piece)


def own_product(fields, spec, blocks, q, at, piece):
    cells = slice(q * piece + at.start, q * piece + at.stop)
    planes = product(fields[0, :, at], fields[1, :, at], *(x[:, at].astype(f32) for x in spec))
    put(blocks, cells.start // LANES, planes)


def near_kernel(place, probe, left, own_spec, right, col, blocks, lines, fields, tails, sems):
    specs = (left, own_spec, right)
    modes, _, rows, width = probe.shape
    piece = width // PIECES
    per = piece // LANES

    def fetch(m, q):
        return pltpu.make_async_copy(probe.at[m, :, :, piece_columns(place, q, piece)], fields.at[m, q], sems.at[m, q])

    order = [(m, q) for m in range(modes) for q in range(len(specs))]
    for m, q in order:
        fetch(m, q).start()
    for m in range(modes):
        for q, spec in enumerate(specs):
            fetch(m, q).wait()
            for at in chunks(piece):
                own_product(fields.at[m, q], [spec.at[0, p] for p in range(2)], blocks.at[m], q, at, piece)
        js = list(range(1, len(specs) * per - 1))
        column_stage(place, blocks.at[m], tails.at[m], col, js, rows, keep_columns(lines.at[m], rows))


def near(place, probe, specs, col):
    modes, _, own, width = probe.shape
    args = [in_hbm(probe)] + [in_vmem(x) for x in (*specs, col)]
    piece = width // PIECES
    return pl.pallas_call(
        near_kernel,
        out_shape=[
            pltpu.VMEM((modes, width // LANES * own, 4 * LANES), bf16),
            pltpu.VMEM((modes, 2, 2 * own, width), bf16),
        ],
        in_specs=[SMEM, HBM] + [VMEM] * (len(args) - 1),
        out_specs=[VMEM] * 2,
        scratch_shapes=[
            pltpu.VMEM((modes, len(specs), 2, own, piece), f32),
            pltpu.VMEM((modes, len(specs) * piece // LANES * own, 2 * LANES), bf16),
            pltpu.SemaphoreType.DMA((modes, len(specs))),
        ],
        compiler_params=pltpu.CompilerParams(vmem_limit_bytes=20 * 1024 * 1024),
        cost_estimate=pl.CostEstimate(flops=6 * 10**9, bytes_accessed=10**7, transcendentals=0),
        name="near",
    )(place, *args)


def first_kernel(place, probe, cross, inner, near_cross, near_inner, far_cross, far_inner, far_spec, high, low, col, _b, _l, *refs):
    wave, blocks, lines, strips, fields, edge_rows, outer, outer_lines, tails, outer_tails, sems, strip_sems = refs
    modes, _, rows, width = probe.shape
    piece = width // PIECES
    per = piece // LANES
    far = PIECES - 1
    edge = 2 * OUTER
    odd = place[ODD]
    keep = [place[UP].astype(f32), place[DOWN].astype(f32)]

    def fetch(m, q):
        at = piece_columns(place, q, piece)
        copies = [
            pltpu.make_async_copy(source.at[m, :, :, at], edge_rows.at[to, m, q], sems.at[k, m, q])
            for k, (source, to) in enumerate(((cross, odd), (inner, 1 - odd)))
        ]
        if q == far:
            copies.append(pltpu.make_async_copy(probe.at[m, :, :, at], fields.at[m], sems.at[2, m, 0]))
        return copies

    strip_copies = []
    for k, (source, to, q) in enumerate(((near_cross, odd, 0), (near_inner, 1 - odd, 0), (far_cross, odd, far), (far_inner, 1 - odd, far))):
        strip_copies.append(pltpu.make_async_copy(source, strips.at[to, q : q + source.shape[0]], strip_sems.at[k]))
    order = [far] + list(range(far))
    for copy in strip_copies:
        copy.start()
    for m in range(modes):
        for q in order:
            for copy in fetch(m, q):
                copy.start()
    for copy in strip_copies:
        copy.wait()
    for m in range(modes):
        for q in order:
            for copy in fetch(m, q):
                copy.wait()
            for at in chunks(piece):
                if q == far:
                    own_product(fields.at[m], (far_spec.at[0], far_spec.at[1]), blocks.at[m], q, at, piece)
                planes = [
                    product(*(edge_rows[e, m, q, p, :, at] for p in range(2)), *(strips[e, q, p, INNER:, at].astype(f32) * keep[e] for p in range(2)))
                    for e in range(2)
                ]
                put(outer.at[m], (q * piece + at.start) // LANES, [jnp.concatenate([planes[0][p], planes[1][p]], axis=0) for p in range(2)])
        js = list(range(far * per - 1, PIECES * per + 1))
        column_stage(place, blocks.at[m], tails.at[m], col, js, rows, keep_columns(lines.at[m], rows))
        column_stage(place, outer.at[m], outer_tails.at[m], col, list(range(PIECES * per)), edge, keep_columns(outer_lines.at[m], edge))
        for at in chunks(width):
            x = [jnp.concatenate([lines[m, k, :, at], outer_lines[m, k, :, at]], axis=0) for k in range(2)]
            wave[m, :, at] = row_stage(*x, high, low)


def first_slice(place, probe, halos, strips, far, bands, blocks, lines):
    modes, _, own, width = probe.shape
    piece = width // PIECES
    anywhere = [*halos, *strips]
    args = [in_hbm(probe), *anywhere] + [in_vmem(x) for x in (far, *bands, blocks, lines)]
    edge = 2 * OUTER
    total = width // LANES
    return pl.pallas_call(
        first_kernel,
        out_shape=[
            pltpu.VMEM((modes, 2 * own + 4 * INNER, width), f32),
            pltpu.VMEM(blocks.shape, bf16),
            pltpu.VMEM(lines.shape, bf16),
            pltpu.VMEM((2, PIECES, *strips[0].shape[1:]), bf16),
        ],
        in_specs=[SMEM, HBM] + [pl.BlockSpec(memory_space=pl.ANY)] * len(anywhere) + [VMEM] * (len(args) - 1 - len(anywhere)),
        out_specs=[VMEM] * 4,
        input_output_aliases={len(args) - 1: 1, len(args): 2},
        scratch_shapes=[
            pltpu.VMEM((modes, 2, own, piece), f32),
            pltpu.VMEM((2, modes, PIECES, 2, OUTER, piece), f32),
            pltpu.VMEM((modes, total * edge, 4 * LANES), bf16),
            pltpu.VMEM((modes, 2, 2 * edge, width), bf16),
            pltpu.VMEM((modes, (total // PIECES + 2) * own, 2 * LANES), bf16),
            pltpu.VMEM((modes, total * edge, 2 * LANES), bf16),
            pltpu.SemaphoreType.DMA((3, modes, PIECES)),
            pltpu.SemaphoreType.DMA((4,)),
        ],
        compiler_params=pltpu.CompilerParams(vmem_limit_bytes=28 * 1024 * 1024),
        name="first_slice",
    )(place, *args)


def second_kernel(place, wave, left, own_spec, right, far_spec, strips, high, low, col, out, blocks, tails, stage, sems):
    modes, _, rows, width = out.shape
    piece = width // PIECES
    per = piece // LANES
    keep = [place[UP].astype(f32), place[DOWN].astype(f32)]
    specs = [[x.at[1, p] for p in range(2)] for x in (left, own_spec, right)] + [[far_spec.at[0], far_spec.at[1]]]

    def leave(m, q):
        at = slice(q * piece, (q + 1) * piece)
        return pltpu.make_async_copy(stage.at[m, :, :, at], out.at[m, :, :, piece_columns(place, q, piece)], sems.at[m, q])

    for m in range(modes):
        for q in range(PIECES):
            for at in chunks(piece):
                cells = slice(q * piece + at.start, q * piece + at.stop)
                inside = product(wave[m, :rows, cells], wave[m, rows : 2 * rows, cells], *(x[:, at].astype(f32) for x in specs[q]))
                edge = [jnp.concatenate([strips[e, q, p, :INNER, at].astype(f32) * keep[e] for e in range(2)], axis=0) for p in range(2)]
                first = 2 * rows
                outside = product(wave[m, first : first + 2 * INNER, cells], wave[m, first + 2 * INNER :, cells], *edge)
                result = row_stage(*split(jnp.concatenate([*inside, *outside], axis=0)), high, low)
                put(blocks.at[m], cells.start // LANES, (result[:rows], result[rows:]))

        def emit(j, real, imag, m=m):
            stage[m, 0, :, lanes(j)] = real
            stage[m, 1, :, lanes(j)] = imag
            if j % per == per - 1:
                leave(m, j // per).start()

        column_stage(place, blocks.at[m], tails.at[m], col, list(range(PIECES * per)), rows, emit)
    for m in range(modes):
        for q in range(PIECES):
            leave(m, q).wait()


def second_slice(place, wave, specs, strips, bands, own):
    modes, _, width = wave.shape
    args = [in_vmem(x) for x in (wave, *specs, strips, *bands)]
    shape = (modes, 2, own, width)
    total = width // LANES
    return pl.pallas_call(
        second_kernel,
        out_shape=jax.ShapeDtypeStruct(shape, f32),
        in_specs=[SMEM] + [VMEM] * len(args),
        out_specs=HBM,
        scratch_shapes=[
            pltpu.VMEM((modes, total * own, 4 * LANES), bf16),
            pltpu.VMEM((modes, total * own, 2 * LANES), bf16),
            pltpu.VMEM(shape, f32),
            pltpu.SemaphoreType.DMA((modes, PIECES)),
        ],
        compiler_params=pltpu.CompilerParams(vmem_limit_bytes=28 * 1024 * 1024),
        name="second_slice",
    )(place, *args)


def turn(x, axis, by):
    n = lax.axis_size(axis)
    return lax.ppermute(x, axis, [(i, (i + by) % n) for i in range(n)])


def swap(x, first):
    n = lax.axis_size("space")
    pairs = [(i, i + 1) for i in range(first, n - 1, 2)]
    return lax.ppermute(x, "space", pairs + [(j, i) for i, j in pairs])


def on_device(probe, specimen, kernels):
    own = probe.shape[2]
    space, mode = lax.axis_index("space"), lax.axis_index("mode")
    odd = space % 2
    place = jnp.stack([mode, odd, (space > 0).astype(jnp.int32), (space < lax.axis_size("space") - 1).astype(jnp.int32)])
    left, right = turn(specimen, "mode", 1), turn(specimen, "mode", -1)
    cross = swap(edges(True, place, probe), 1)
    inner = swap(edges(False, place, probe), 0)
    *bands0, band1h, band1l, col = prepare(kernels, own)
    left, right, col = lax.optimization_barrier((left, right, col))
    far0, far1 = turn(left[0], "mode", 1), turn(right[1], "mode", -1)

    def strips(specs):
        last = jnp.stack([jnp.concatenate([x[1][:, own - INNER :], x[0][:, own - OUTER :]], axis=1) for x in specs])
        first = jnp.stack([jnp.concatenate([x[1][:, :INNER], x[0][:, :OUTER]], axis=1) for x in specs])
        return swap(jnp.where(odd == 1, last, first), 1), swap(jnp.where(odd == 1, first, last), 0)

    left_here, right_here, inner = lax.optimization_barrier((left, right, inner))
    near_cross, near_inner = strips([left_here, specimen, right_here])
    blocks, lines = near(place, probe, [left, specimen, right], col)
    far0, far1, blocks, lines, near_inner = lax.optimization_barrier((far0, far1, blocks, lines, near_inner))
    far_cross, far_inner = strips([(far0, far1)])
    all_strips = (near_cross, near_inner, far_cross, far_inner)
    wave, _, _, edge_strips = first_slice(place, probe, (cross, inner), all_strips, far0, (*bands0, col), blocks, lines)
    specs = (left, specimen, right, far1)
    return second_slice(place, wave, specs, edge_strips, (band1h, band1l, col), own)


def solution(mesh):
    return jax.shard_map(
        on_device,
        mesh=mesh,
        in_specs=(P("mode", None, "space", None), P(None, None, "space", "mode"), P()),
        out_specs=P("mode", None, "space", None),
        check_vma=False,
    )
```

profile of v0, /device:TPU:71, one launch (start us, length us, event | category | flops | bytes accessed | tf_op | source)
XLA Modules:
  0.0 60.5 jit_solution(15623649462330434490)
XLA Ops:
  0.0 0.1 pad_add_fusion.place
  0.1 2.7 %edges_inner.1 = f32[2,2,24,4096]{3,2,1,0:T(8,128)} custom-call(s32[4]{0:T(128)S(1)} %pad_add_fusion.place, f32[2,2,64,4096]{3,2,1,0:T(8,128)} %probe.7), custom_call_target="tpu_custom_call" | custom-call | tf_op jit(solution)/shard_map/edges_inner/pallas_call | solution.py:100
  2.8 0.0 copy-start.1
  2.8 0.8 %collective-permute-start.3 = (f32[2,2,24,4096]{3,2,1,0:T(8,128)}, f32[2,2,24,4096]{3,2,1,0:T(8,128)}, u32[]{:S(2)}, u32[]{:S(2)}) collective-permute-start(f32[2,2,24,4096]{3,2,1,0:T(8,128)} %edges_inner.1), channel_id=1, source_target_pairs={{0,4},{8,12},{16,20},{24,28},{32,36},{40,44},{48,52},{56,60},{64,6... | collective-permute-start | bytes 4718600 | tf_op jit(solution)/shard_map/ppermute | solution.py:434
  3.6 0.0 copy-done
  3.6 2.7 %collective-permute-start.2 = (bf16[2,2,64,1024]{3,2,1,0:T(8,128)(2,1)S(1)}, bf16[2,2,64,1024]{3,2,1,0:T(8,128)(2,1)S(1)}, u32[]{:S(2)}, u32[]{:S(2)}) collective-permute-start(bf16[2,2,64,1024]{3,2,1,0:T(8,128)(2,1)S(1)} %copy-done), channel_id=1, source_target_pairs={{0,3},{1,0},{2,1},{3,2},{4,7},{5,4},{6,5},{7,6},{8,11},{9,8},{10,9... | collective-permute-start | bytes 1572872 | tf_op jit(solution)/shard_map/ppermute | solution.py:428
  6.4 0.0 collective-permute-start.1
  6.4 2.4 %edges_cross.1 = f32[2,2,24,4096]{3,2,1,0:T(8,128)S(1)} custom-call(s32[4]{0:T(128)S(1)} %pad_add_fusion.place, f32[2,2,64,4096]{3,2,1,0:T(8,128)} %probe.7), custom_call_target="tpu_custom_call" | custom-call | tf_op jit(solution)/shard_map/edges_cross/pallas_call | solution.py:100
  8.7 3.4 %collective-permute-start = (f32[2,2,24,4096]{3,2,1,0:T(8,128)S(1)}, f32[2,2,24,4096]{3,2,1,0:T(8,128)}, u32[]{:S(2)}, u32[]{:S(2)}) collective-permute-start(f32[2,2,24,4096]{3,2,1,0:T(8,128)S(1)} %edges_cross.1), channel_id=1, source_target_pairs={{4,8},{12,16},{20,24},{28,32},{36,40},{44,48},{52,56},{60,64},{68,... | collective-permute-start | bytes 4718600 | tf_op jit(solution)/shard_map/ppermute | solution.py:434
  12.2 2.5 %prepare.1 = (bf16[192,224]{1,0:T(8,128)(2,1)S(1)}, bf16[192,224]{1,0:T(8,128)(2,1)S(1)}, bf16[128,192]{1,0:T(8,128)(2,1)S(1)}, bf16[128,192]{1,0:T(8,128)(2,1)S(1)}, bf16[1024,256]{1,0:T(8,128)(2,1)S(1)}) custom-call(f32[2,2,24]{2,1,0:T(2,128)S(1)} %copy-done.1), custom_call_target="tpu_custom_call" | custom-call | tf_op jit(solution)/shard_map/prepare/pallas_call | solution.py:137
  14.7 2.9 %collective-permute-done.2.right = bf16[2,2,64,1024]{3,2,1,0:T(8,128)(2,1)S(1)} collective-permute-done((bf16[2,2,64,1024]{3,2,1,0:T(8,128)(2,1)S(1)}, bf16[2,2,64,1024]{3,2,1,0:T(8,128)(2,1)S(1)}, u32[]{:S(2)}, u32[]{:S(2)}) %collective-permute-start.2) | collective-permute-done | bytes 524320 | tf_op jit(solution)/shard_map/ppermute | solution.py:428
  17.6 3.1 %collective-permute-done.1.left = bf16[2,2,64,1024]{3,2,1,0:T(8,128)(2,1)S(1)} collective-permute-done((bf16[2,2,64,1024]{3,2,1,0:T(8,128)(2,1)S(1)}, bf16[2,2,64,1024]{3,2,1,0:T(8,128)(2,1)S(1)}, u32[]{:S(2)}, u32[]{:S(2)}) %collective-permute-start.1) | collective-permute-done | bytes 524320 | tf_op jit(solution)/shard_map/ppermute | solution.py:428
  20.7 0.4 collective-permute-start.6
  21.1 1.2 %collective-permute-start.5 = (bf16[2,64,1024]{2,1,0:T(8,128)(2,1)S(1)}, bf16[2,64,1024]{2,1,0:T(8,128)(2,1)S(1)}, u32[]{:S(2)}, u32[]{:S(2)}) collective-permute-start(bf16[2,64,1024]{2,1,0:T(8,128)(2,1)S(1)} %slice_bitcast_fusion.1), channel_id=1, source_target_pairs={{0,1},{1,2},{2,3},{3,0},{4,5},{5,6},{6,7},{7,4},{8,9},{9,10},{10,1... | collective-permute-start | bytes 786440 | tf_op jit(solution)/shard_map/ppermute | solution.py:428
  22.4 0.0 collective-permute-done.3.inner
  22.4 0.1 slice_bitcast_fusion.3
  22.6 0.1 broadcast_select_fusion
  22.8 1.8 %collective-permute-start.7 = (bf16[3,2,40,1024]{3,2,1,0:T(8,128)(2,1)S(1)}, bf16[3,2,40,1024]{3,2,1,0:T(8,128)(2,1)S(1)}, u32[]{:S(2)}, u32[]{:S(2)}) collective-permute-start(bf16[3,2,40,1024]{3,2,1,0:T(8,128)(2,1)S(1)} %get-tuple-element.45), channel_id=1, source_target_pairs={{0,4},{8,12},{16,20},{24,28},{32,36},{40,44},{48,52},{56,60},{64,6... | collective-permute-start | bytes 1474568 | tf_op jit(solution)/shard_map/ppermute | solution.py:434
  24.6 4.8 %near.1 = (bf16[2,2048,512]{2,1,0:T(8,128)(2,1)S(1)}, bf16[2,2,128,4096]{3,2,1,0:T(8,128)(2,1)S(1)}) custom-call(s32[4]{0:T(128)S(1)} %pad_add_fusion.place, f32[2,2,64,4096]{3,2,1,0:T(8,128)} %probe.7, bf16[2,2,64,1024]{3,2,1,0:T(8,128)(2,1)S(1)} %collective-permute-done.1.left, bf16[2,2,64,1024]{3,2,1,0:T(8,128)(2,1)S(1)} %copy-done, ...), custom_call_target="tpu_custom_call" | custom-call | flops 6000000000 | bytes 10000000 | tf_op jit(solution)/shard_map/near/pallas_call | solution.py:267
  29.4 3.1 %collective-permute-start.4 = (bf16[3,2,40,1024]{3,2,1,0:T(8,128)(2,1)S(1)}, bf16[3,2,40,1024]{3,2,1,0:T(8,128)(2,1)S(1)}, u32[]{:S(2)}, u32[]{:S(2)}) collective-permute-start(bf16[3,2,40,1024]{3,2,1,0:T(8,128)(2,1)S(1)} %get-tuple-element.46), channel_id=1, source_target_pairs={{4,8},{12,16},{20,24},{28,32},{36,40},{44,48},{52,56},{60,64},{68,... | collective-permute-start | bytes 1474568 | tf_op jit(solution)/shard_map/ppermute | solution.py:434
  32.5 0.0 collective-permute-done.6.far_spec
  32.5 0.0 collective-permute-done.5.far_spec
  32.5 0.0 collective-permute-done.7.near_inner
  32.6 0.1 broadcast_select_fusion.2
  32.6 0.1 collective-permute-start.9
  32.7 4.8 %collective-permute-start.8 = (bf16[1,2,40,1024]{3,2,1,0:T(8,128)(2,1)S(1)}, bf16[1,2,40,1024]{3,2,1,0:T(8,128)(2,1)S(1)}, u32[]{:S(2)}, u32[]{:S(2)}) collective-permute-start(bf16[1,2,40,1024]{3,2,1,0:T(8,128)(2,1)S(1)} %get-tuple-element.54), channel_id=1, source_target_pairs={{4,8},{12,16},{20,24},{28,32},{36,40},{44,48},{52,56},{60,64},{68,... | collective-permute-start | bytes 491528 | tf_op jit(solution)/shard_map/ppermute | solution.py:434
  37.5 0.0 collective-permute-done.cross
  37.5 4.1 %collective-permute-done.4.near_cross = bf16[3,2,40,1024]{3,2,1,0:T(8,128)(2,1)S(1)} collective-permute-done((bf16[3,2,40,1024]{3,2,1,0:T(8,128)(2,1)S(1)}, bf16[3,2,40,1024]{3,2,1,0:T(8,128)(2,1)S(1)}, u32[]{:S(2)}, u32[]{:S(2)}) %collective-permute-start.4) | collective-permute-done | bytes 491552 | tf_op jit(solution)/shard_map/ppermute | solution.py:434
  41.7 0.0 collective-permute-done.9.far_inner
  41.7 1.8 %collective-permute-done.8.far_cross = bf16[1,2,40,1024]{3,2,1,0:T(8,128)(2,1)S(1)} collective-permute-done((bf16[1,2,40,1024]{3,2,1,0:T(8,128)(2,1)S(1)}, bf16[1,2,40,1024]{3,2,1,0:T(8,128)(2,1)S(1)}, u32[]{:S(2)}, u32[]{:S(2)}) %collective-permute-start.8) | collective-permute-done | bytes 163872 | tf_op jit(solution)/shard_map/ppermute | solution.py:434
  43.4 10.1 %first_slice.1 = (f32[2,192,4096]{2,1,0:T(8,128)S(1)}, bf16[2,2048,512]{2,1,0:T(8,128)(2,1)S(1)}, bf16[2,2,128,4096]{3,2,1,0:T(8,128)(2,1)S(1)}, bf16[2,4,2,40,1024]{4,3,2,1,0:T(8,128)(2,1)S(1)}) custom-call(s32[4]{0:T(128)S(1)} %pad_add_fusion.place, f32[2,2,64,4096]{3,2,1,0:T(8,128)} %probe.7, ...), custom_call_target="tpu_custom_call", output_to_operand_aliasing={{1}: (12, {}), {2}: (13, {})} | custom-call | tf_op jit(solution)/shard_map/first_slice/pallas_call | solution.py:345
  53.5 6.8 %second_slice.1 = f32[2,2,64,4096]{3,2,1,0:T(8,128)} custom-call(s32[4]{0:T(128)S(1)} %pad_add_fusion.place, f32[2,192,4096]{2,1,0:T(8,128)S(1)} %get-tuple-element.41.wave, bf16[2,2,64,1024]{3,2,1,0:T(8,128)(2,1)S(1)} %collective-permute-done.1.left, bf16[2,2,64,1024]{3,2,1,0:T(8,128)(2,1)S(1)} %copy-done, ...), custom_call_target="tpu_custom_call" | custom-call | tf_op jit(solution)/shard_map/second_slice/pallas_call | solution.py:410
  (18 shorter events, 0.3 us)
Async XLA Ops:
  0.0 3.6 %copy-start = (bf16[2,2,64,1024]{3,2,1,0:T(8,128)(2,1)S(1)}, bf16[2,2,64,1024]{3,2,1,0:T(8,128)(2,1)}, u32[]{:S(2)}) copy-start(bf16[2,2,64,1024]{3,2,1,0:T(8,128)(2,1)} %own_spec.3) | copy-start | bytes 1572868
  2.8 9.3 %copy-start.1 = (f32[2,2,24]{2,1,0:T(2,128)S(1)}, f32[2,2,24]{2,1,0:T(2,128)}, u32[]{:S(2)}) copy-start(f32[2,2,24]{2,1,0:T(2,128)} %kernels.1) | copy-start | bytes 1156
  2.8 19.5 %collective-permute-start.3 = (f32[2,2,24,4096]{3,2,1,0:T(8,128)}, f32[2,2,24,4096]{3,2,1,0:T(8,128)}, u32[]{:S(2)}, u32[]{:S(2)}) collective-permute-start(f32[2,2,24,4096]{3,2,1,0:T(8,128)} %edges_inner.1), channel_id=1, source_target_pairs={{0,4},{8,12},{16,20},{24,28},{32,36},{40,44},{48,52},{56,60},{64,6... | collective-permute-start | bytes 4718600 | tf_op jit(solution)/shard_map/ppermute | solution.py:434
  3.6 14.0 %collective-permute-start.2 = (bf16[2,2,64,1024]{3,2,1,0:T(8,128)(2,1)S(1)}, bf16[2,2,64,1024]{3,2,1,0:T(8,128)(2,1)S(1)}, u32[]{:S(2)}, u32[]{:S(2)}) collective-permute-start(bf16[2,2,64,1024]{3,2,1,0:T(8,128)(2,1)S(1)} %copy-done), channel_id=1, source_target_pairs={{0,3},{1,0},{2,1},{3,2},{4,7},{5,4},{6,5},{7,6},{8,11},{9,8},{10,9... | collective-permute-start | bytes 1572872 | tf_op jit(solution)/shard_map/ppermute | solution.py:428
  6.4 14.4 %collective-permute-start.1 = (bf16[2,2,64,1024]{3,2,1,0:T(8,128)(2,1)S(1)}, bf16[2,2,64,1024]{3,2,1,0:T(8,128)(2,1)S(1)}, u32[]{:S(2)}, u32[]{:S(2)}) collective-permute-start(bf16[2,2,64,1024]{3,2,1,0:T(8,128)(2,1)S(1)} %copy-done), channel_id=1, source_target_pairs={{0,1},{1,2},{2,3},{3,0},{4,5},{5,6},{6,7},{7,4},{8,9},{9,10},{10,1... | collective-permute-start | bytes 1572872 | tf_op jit(solution)/shard_map/ppermute | solution.py:428
  8.7 28.8 %collective-permute-start = (f32[2,2,24,4096]{3,2,1,0:T(8,128)S(1)}, f32[2,2,24,4096]{3,2,1,0:T(8,128)}, u32[]{:S(2)}, u32[]{:S(2)}) collective-permute-start(f32[2,2,24,4096]{3,2,1,0:T(8,128)S(1)} %edges_cross.1), channel_id=1, source_target_pairs={{4,8},{12,16},{20,24},{28,32},{36,40},{44,48},{52,56},{60,64},{68,... | collective-permute-start | bytes 4718600 | tf_op jit(solution)/shard_map/ppermute | solution.py:434
  20.7 11.7 %collective-permute-start.6 = (bf16[2,64,1024]{2,1,0:T(8,128)(2,1)S(1)}, bf16[2,64,1024]{2,1,0:T(8,128)(2,1)S(1)}, u32[]{:S(2)}, u32[]{:S(2)}) collective-permute-start(bf16[2,64,1024]{2,1,0:T(8,128)(2,1)S(1)} %slice_bitcast_fusion), channel_id=1, source_target_pairs={{0,3},{1,0},{2,1},{3,2},{4,7},{5,4},{6,5},{7,6},{8,11},{9,8},{10,9... | collective-permute-start | bytes 786440 | tf_op jit(solution)/shard_map/ppermute | solution.py:428
  21.1 11.3 %collective-permute-start.5 = (bf16[2,64,1024]{2,1,0:T(8,128)(2,1)S(1)}, bf16[2,64,1024]{2,1,0:T(8,128)(2,1)S(1)}, u32[]{:S(2)}, u32[]{:S(2)}) collective-permute-start(bf16[2,64,1024]{2,1,0:T(8,128)(2,1)S(1)} %slice_bitcast_fusion.1), channel_id=1, source_target_pairs={{0,1},{1,2},{2,3},{3,0},{4,5},{5,6},{6,7},{7,4},{8,9},{9,10},{10,1... | collective-permute-start | bytes 786440 | tf_op jit(solution)/shard_map/ppermute | solution.py:428
  22.8 9.7 %collective-permute-start.7 = (bf16[3,2,40,1024]{3,2,1,0:T(8,128)(2,1)S(1)}, bf16[3,2,40,1024]{3,2,1,0:T(8,128)(2,1)S(1)}, u32[]{:S(2)}, u32[]{:S(2)}) collective-permute-start(bf16[3,2,40,1024]{3,2,1,0:T(8,128)(2,1)S(1)} %get-tuple-element.45), channel_id=1, source_target_pairs={{0,4},{8,12},{16,20},{24,28},{32,36},{40,44},{48,52},{56,60},{64,6... | collective-permute-start | bytes 1474568 | tf_op jit(solution)/shard_map/ppermute | solution.py:434
  29.4 12.3 %collective-permute-start.4 = (bf16[3,2,40,1024]{3,2,1,0:T(8,128)(2,1)S(1)}, bf16[3,2,40,1024]{3,2,1,0:T(8,128)(2,1)S(1)}, u32[]{:S(2)}, u32[]{:S(2)}) collective-permute-start(bf16[3,2,40,1024]{3,2,1,0:T(8,128)(2,1)S(1)} %get-tuple-element.46), channel_id=1, source_target_pairs={{4,8},{12,16},{20,24},{28,32},{36,40},{44,48},{52,56},{60,64},{68,... | collective-permute-start | bytes 1474568 | tf_op jit(solution)/shard_map/ppermute | solution.py:434
  32.6 9.0 %collective-permute-start.9 = (bf16[1,2,40,1024]{3,2,1,0:T(8,128)(2,1)S(1)}, bf16[1,2,40,1024]{3,2,1,0:T(8,128)(2,1)S(1)}, u32[]{:S(2)}, u32[]{:S(2)}) collective-permute-start(bf16[1,2,40,1024]{3,2,1,0:T(8,128)(2,1)S(1)} %get-tuple-element.53), channel_id=1, source_target_pairs={{0,4},{8,12},{16,20},{24,28},{32,36},{40,44},{48,52},{56,60},{64,6... | collective-permute-start | bytes 491528 | tf_op jit(solution)/shard_map/ppermute | solution.py:434
  32.7 10.7 %collective-permute-start.8 = (bf16[1,2,40,1024]{3,2,1,0:T(8,128)(2,1)S(1)}, bf16[1,2,40,1024]{3,2,1,0:T(8,128)(2,1)S(1)}, u32[]{:S(2)}, u32[]{:S(2)}) collective-permute-start(bf16[1,2,40,1024]{3,2,1,0:T(8,128)(2,1)S(1)} %get-tuple-element.54), channel_id=1, source_target_pairs={{4,8},{12,16},{20,24},{28,32},{36,40},{44,48},{52,56},{60,64},{68,... | collective-permute-start | bytes 491528 | tf_op jit(solution)/shard_map/ppermute | solution.py:434
where the time goes:
time: 60.7 us; the launch traced here: 60.5 us
  Pallas kernels  29.3 us (48%)
  starting transfers between devices  18.3 us (30%)
  waiting for transfers between devices  11.9 us (20%)
    ppermute x6, starting transfers between devices, swap(): return lax.ppermute(x, 'space', pairs + [(j, i) for i, j in pairs])  13.9 us
    pallas_call x1, Pallas kernels, first_slice(): pl.pallas_call(first_kernel, out_shape=[pltpu.VMEM((modes, 2 * own + 4 *...  10.1 us
    pallas_call x1, Pallas kernels, second_slice(): pl.pallas_call(second_kernel, out_shape=jax.ShapeDtypeStruct(shape, f32),...  6.82 us
    ppermute x4, waiting for transfers between devices, turn(): return lax.ppermute(x, axis, [(i, (i + by) % n) for i in range(n)])  5.98 us
    ppermute x6, waiting for transfers between devices, swap(): return lax.ppermute(x, 'space', pairs + [(j, i) for i, j in pairs])  5.91 us
    pallas_call x2, Pallas kernels, edges(): pl.pallas_call(functools.partial(edges_kernel, for_odd), out_shape=jax.Sh...  5.1 us
    pallas_call x1, Pallas kernels, near(): pl.pallas_call(near_kernel, out_shape=[pltpu.VMEM((modes, width // LANES...  4.8 us
    ppermute x4, starting transfers between devices, turn(): return lax.ppermute(x, axis, [(i, (i + by) % n) for i in range(n)])  4.36 us
  transfers between devices with their start and end apart: 10, of which 4 were waited for; matrix products, arithmetic and copies ran while one was open for 1% of the time, Pallas kernels for 16%

commit v1 on v0

--- a/solution.py
+++ b/solution.py
@@ -239,141 +239,144 @@
     put(blocks, cells.start // LANES, planes)
 
 
-def near_kernel(place, probe, left, own_spec, right, col, blocks, lines, fields, tails, sems):
-    specs = (left, own_spec, right)
+def own_kernel(tasks, edges_too, place, probe, *refs):
+    n = 1 + max(q for _, pieces, _ in tasks for q in pieces)
+    specs, col = refs[:n], refs[n]
+    if edges_too:
+        cross, inner = refs[n + 1 : n + 3]
+        blocks, lines, edge_rows, fields, tails, sems, edge_sems = refs[n + 5 :]
+    else:
+        blocks, lines, fields, tails, sems = refs[n + 1 :]
     modes, _, rows, width = probe.shape
     piece = width // PIECES
-    per = piece // LANES
-
-    def fetch(m, q):
-        return pltpu.make_async_copy(probe.at[m, :, :, piece_columns(place, q, piece)], fields.at[m, q], sems.at[m, q])
-
-    order = [(m, q) for m in range(modes) for q in range(len(specs))]
-    for m, q in order:
-        fetch(m, q).start()
-    for m in range(modes):
-        for q, spec in enumerate(specs):
-            fetch(m, q).wait()
+    odd = place[ODD]
+
+    def fetch(k, m, q):
+        return pltpu.make_async_copy(probe.at[m, :, :, piece_columns(place, q, piece)], fields.at[k], sems.at[k])
+
+    order = [(m, q) for m, pieces, _ in tasks for q in pieces]
+    for k, (m, q) in enumerate(order):
+        fetch(k, m, q).start()
+    copies = []
+    if edges_too:
+        for m in range(modes):
+            for q in range(PIECES):
+                at = piece_columns(place, q, piece)
+                for e, (source, to) in enumerate(((cross, odd), (inner, 1 - odd))):
+                    copies.append(pltpu.make_async_copy(source.at[m, :, :, at], edge_rows.at[to, m, q], edge_sems.at[e, m, q]))
+    for copy in copies:
+        copy.start()
+    k = 0
+    for t, (m, pieces, js) in enumerate(tasks):
+        for q in pieces:
+            fetch(k, m, q).wait()
+            spec = [specs[q].at[0, p] if q < PIECES - 1 else specs[q].at[p] for p in range(2)]
             for at in chunks(piece):
-                own_product(fields.at[m, q], [spec.at[0, p] for p in range(2)], blocks.at[m], q, at, piece)
-        js = list(range(1, len(specs) * per - 1))
-        column_stage(place, blocks.at[m], tails.at[m], col, js, rows, keep_columns(lines.at[m], rows))
-
-
-def near(place, probe, specs, col):
+                own_product(fields.at[k], spec, blocks.at[m], q, at, piece)
+            k += 1
+        column_stage(place, blocks.at[m], tails.at[t], col, js, rows, keep_columns(lines.at[m], rows))
+    for copy in copies:
+        copy.wait()
+
+
+def own_rows(tasks, place, probe, specs, col, halos=(), made=()):
     modes, _, own, width = probe.shape
-    args = [in_hbm(probe)] + [in_vmem(x) for x in (*specs, col)]
+    args = [in_hbm(probe)] + [in_vmem(x) for x in (*specs, col)] + [*halos] + [in_vmem(x) for x in made]
     piece = width // PIECES
+    fetches = sum(len(pieces) for _, pieces, _ in tasks)
+    longest = max(len(js) for _, _, js in tasks)
+    out = [
+        pltpu.VMEM((modes, width // LANES * own, 4 * LANES), bf16),
+        pltpu.VMEM((modes, 2, 2 * own, width), bf16),
+    ]
+    scratch = [
+        pltpu.VMEM((fetches, 2, own, piece), f32),
+        pltpu.VMEM((len(tasks), longest * own, 2 * LANES), bf16),
+        pltpu.SemaphoreType.DMA((fetches,)),
+    ]
+    if halos:
+        out.append(pltpu.VMEM((2, modes, PIECES, 2, OUTER, piece), f32))
+        scratch.append(pltpu.SemaphoreType.DMA((2, modes, PIECES)))
+    first = 1 + len(args) - len(made)
     return pl.pallas_call(
-        near_kernel,
-        out_shape=[
-            pltpu.VMEM((modes, width // LANES * own, 4 * LANES), bf16),
-            pltpu.VMEM((modes, 2, 2 * own, width), bf16),
-        ],
-        in_specs=[SMEM, HBM] + [VMEM] * (len(args) - 1),
-        out_specs=[VMEM] * 2,
-        scratch_shapes=[
-            pltpu.VMEM((modes, len(specs), 2, own, piece), f32),
-            pltpu.VMEM((modes, len(specs) * piece // LANES * own, 2 * LANES), bf16),
-            pltpu.SemaphoreType.DMA((modes, len(specs))),
-        ],
+        functools.partial(own_kernel, tasks, bool(halos)),
+        out_shape=out,
+        in_specs=[SMEM, HBM] + [VMEM] * (1 + len(specs)) + [pl.BlockSpec(memory_space=pl.ANY)] * len(halos) + [VMEM] * len(made),
+        out_specs=[VMEM] * len(out),
+        input_output_aliases={first + k: k for k in range(len(made))},
+        scratch_shapes=scratch,
         compiler_params=pltpu.CompilerParams(vmem_limit_bytes=20 * 1024 * 1024),
-        cost_estimate=pl.CostEstimate(flops=6 * 10**9, bytes_accessed=10**7, transcendentals=0),
-        name="near",
+        cost_estimate=pl.CostEstimate(flops=4 * 10**9, bytes_accessed=10**7, transcendentals=0),
+        name="own_rest" if halos else "own_near",
     )(place, *args)
 
 
-def first_kernel(place, probe, cross, inner, near_cross, near_inner, far_cross, far_inner, far_spec, high, low, col, _b, _l, *refs):
-    wave, blocks, lines, strips, fields, edge_rows, outer, outer_lines, tails, outer_tails, sems, strip_sems = refs
-    modes, _, rows, width = probe.shape
-    piece = width // PIECES
-    per = piece // LANES
-    far = PIECES - 1
+def first_kernel(place, edge_rows, strips_cross, strips_inner, high, low, col, lines, wave, strips, outer, outer_lines, outer_tails, strip_sems):
+    _, modes, _, _, _, piece = edge_rows.shape
+    width = PIECES * piece
     edge = 2 * OUTER
     odd = place[ODD]
     keep = [place[UP].astype(f32), place[DOWN].astype(f32)]
-
-    def fetch(m, q):
-        at = piece_columns(place, q, piece)
-        copies = [
-            pltpu.make_async_copy(source.at[m, :, :, at], edge_rows.at[to, m, q], sems.at[k, m, q])
-            for k, (source, to) in enumerate(((cross, odd), (inner, 1 - odd)))
-        ]
-        if q == far:
-            copies.append(pltpu.make_async_copy(probe.at[m, :, :, at], fields.at[m], sems.at[2, m, 0]))
-        return copies
-
-    strip_copies = []
-    for k, (source, to, q) in enumerate(((near_cross, odd, 0), (near_inner, 1 - odd, 0), (far_cross, odd, far), (far_inner, 1 - odd, far))):
-        strip_copies.append(pltpu.make_async_copy(source, strips.at[to, q : q + source.shape[0]], strip_sems.at[k]))
-    order = [far] + list(range(far))
+    strip_copies = [
+        pltpu.make_async_copy(source, strips.at[to], strip_sems.at[to])
+        for source, to in ((strips_cross, odd), (strips_inner, 1 - odd))
+    ]
     for copy in strip_copies:
         copy.start()
-    for m in range(modes):
-        for q in order:
-            for copy in fetch(m, q):
-                copy.start()
     for copy in strip_copies:
         copy.wait()
     for m in range(modes):
-        for q in order:
-            for copy in fetch(m, q):
-                copy.wait()
+        for q in range(PIECES):
             for at in chunks(piece):
-                if q == far:
-                    own_product(fields.at[m], (far_spec.at[0], far_spec.at[1]), blocks.at[m], q, at, piece)
                 planes = [
-                    product(*(edge_rows[e, m, q, p, :, at] for p in range(2)), *(strips[e, q, p, INNER:, at].astype(f32) * keep[e] for p in range(2)))
+                    product(*(edge_rows[e, m, q, p, :, at] for p in range(2)), *(strips[e, q, p, :, at].astype(f32) * keep[e] for p in range(2)))
                     for e in range(2)
                 ]
                 put(outer.at[m], (q * piece + at.start) // LANES, [jnp.concatenate([planes[0][p], planes[1][p]], axis=0) for p in range(2)])
-        js = list(range(far * per - 1, PIECES * per + 1))
-        column_stage(place, blocks.at[m], tails.at[m], col, js, rows, keep_columns(lines.at[m], rows))
-        column_stage(place, outer.at[m], outer_tails.at[m], col, list(range(PIECES * per)), edge, keep_columns(outer_lines.at[m], edge))
+        column_stage(place, outer.at[m], outer_tails.at[m], col, list(range(width // LANES)), edge, keep_columns(outer_lines.at[m], edge))
         for at in chunks(width):
             x = [jnp.concatenate([lines[m, k, :, at], outer_lines[m, k, :, at]], axis=0) for k in range(2)]
             wave[m, :, at] = row_stage(*x, high, low)
 
 
-def first_slice(place, probe, halos, strips, far, bands, blocks, lines):
-    modes, _, own, width = probe.shape
-    piece = width // PIECES
-    anywhere = [*halos, *strips]
-    args = [in_hbm(probe), *anywhere] + [in_vmem(x) for x in (far, *bands, blocks, lines)]
+def first_slice(place, edge_rows, strips, bands, lines):
+    modes = lines.shape[0]
+    width = lines.shape[3]
+    args = [in_vmem(edge_rows), *strips] + [in_vmem(x) for x in (*bands, lines)]
     edge = 2 * OUTER
     total = width // LANES
     return pl.pallas_call(
         first_kernel,
-        out_shape=[
-            pltpu.VMEM((modes, 2 * own + 4 * INNER, width), f32),
-            pltpu.VMEM(blocks.shape, bf16),
-            pltpu.VMEM(lines.shape, bf16),
-            pltpu.VMEM((2, PIECES, *strips[0].shape[1:]), bf16),
-        ],
-        in_specs=[SMEM, HBM] + [pl.BlockSpec(memory_space=pl.ANY)] * len(anywhere) + [VMEM] * (len(args) - 1 - len(anywhere)),
-        out_specs=[VMEM] * 4,
-        input_output_aliases={len(args) - 1: 1, len(args): 2},
+        out_shape=pltpu.VMEM((modes, bands[0].shape[0], width), f32),
+        in_specs=[SMEM, VMEM] + [pl.BlockSpec(memory_space=pl.ANY)] * 2 + [VMEM] * (1 + len(bands)),
+        out_specs=VMEM,
         scratch_shapes=[
-            pltpu.VMEM((modes, 2, own, piece), f32),
-            pltpu.VMEM((2, modes, PIECES, 2, OUTER, piece), f32),
+            pltpu.VMEM((2, *strips[0].shape), bf16),
             pltpu.VMEM((modes, total * edge, 4 * LANES), bf16),
             pltpu.VMEM((modes, 2, 2 * edge, width), bf16),
-            pltpu.VMEM((modes, (total // PIECES + 2) * own, 2 * LANES), bf16),
             pltpu.VMEM((modes, total * edge, 2 * LANES), bf16),
-            pltpu.SemaphoreType.DMA((3, modes, PIECES)),
-            pltpu.SemaphoreType.DMA((4,)),
+            pltpu.SemaphoreType.DMA((2,)),
         ],
-        compiler_params=pltpu.CompilerParams(vmem_limit_bytes=28 * 1024 * 1024),
+        compiler_params=pltpu.CompilerParams(vmem_limit_bytes=24 * 1024 * 1024),
         name="first_slice",
     )(place, *args)
 
 
-def second_kernel(place, wave, left, own_spec, right, far_spec, strips, high, low, col, out, blocks, tails, stage, sems):
+def second_kernel(place, wave, left, own_spec, right, far_spec, strips_cross, strips_inner, high, low, col, out, blocks, tails, stage, strips, sems, strip_sems):
     modes, _, rows, width = out.shape
     piece = width // PIECES
     per = piece // LANES
     keep = [place[UP].astype(f32), place[DOWN].astype(f32)]
     specs = [[x.at[1, p] for p in range(2)] for x in (left, own_spec, right)] + [[far_spec.at[0], far_spec.at[1]]]
+    odd = place[ODD]
+    strip_copies = [
+        pltpu.make_async_copy(source, strips.at[to], strip_sems.at[to])
+        for source, to in ((strips_cross, odd), (strips_inner, 1 - odd))
+    ]
+    for copy in strip_copies:
+        copy.start()
+    for copy in strip_copies:
+        copy.wait()
 
     def leave(m, q):
         at = slice(q * piece, (q + 1) * piece)
@@ -384,7 +387,7 @@
             for at in chunks(piece):
                 cells = slice(q * piece + at.start, q * piece + at.stop)
                 inside = product(wave[m, :rows, cells], wave[m, rows : 2 * rows, cells], *(x[:, at].astype(f32) for x in specs[q]))
-                edge = [jnp.concatenate([strips[e, q, p, :INNER, at].astype(f32) * keep[e] for e in range(2)], axis=0) for p in range(2)]
+                edge = [jnp.concatenate([strips[e, q, p, :, at].astype(f32) * keep[e] for e in range(2)], axis=0) for p in range(2)]
                 first = 2 * rows
                 outside = product(wave[m, first : first + 2 * INNER, cells], wave[m, first + 2 * INNER :, cells], *edge)
                 result = row_stage(*split(jnp.concatenate([*inside, *outside], axis=0)), high, low)
@@ -404,19 +407,21 @@
 
 def second_slice(place, wave, specs, strips, bands, own):
     modes, _, width = wave.shape
-    args = [in_vmem(x) for x in (wave, *specs, strips, *bands)]
+    args = [*(in_vmem(x) for x in (wave, *specs)), *strips, *(in_vmem(x) for x in bands)]
     shape = (modes, 2, own, width)
     total = width // LANES
     return pl.pallas_call(
         second_kernel,
         out_shape=jax.ShapeDtypeStruct(shape, f32),
-        in_specs=[SMEM] + [VMEM] * len(args),
+        in_specs=[SMEM] + [VMEM] * (1 + len(specs)) + [pl.BlockSpec(memory_space=pl.ANY)] * 2 + [VMEM] * len(bands),
         out_specs=HBM,
         scratch_shapes=[
             pltpu.VMEM((modes, total * own, 4 * LANES), bf16),
             pltpu.VMEM((modes, total * own, 2 * LANES), bf16),
             pltpu.VMEM(shape, f32),
+            pltpu.VMEM((2, *strips[0].shape), bf16),
             pltpu.SemaphoreType.DMA((modes, PIECES)),
+            pltpu.SemaphoreType.DMA((2,)),
         ],
         compiler_params=pltpu.CompilerParams(vmem_limit_bytes=28 * 1024 * 1024),
         name="second_slice",
@@ -445,21 +450,27 @@
     *bands0, band1h, band1l, col = prepare(kernels, own)
     left, right, col = lax.optimization_barrier((left, right, col))
     far0, far1 = turn(left[0], "mode", 1), turn(right[1], "mode", -1)
-
-    def strips(specs):
-        last = jnp.stack([jnp.concatenate([x[1][:, own - INNER :], x[0][:, own - OUTER :]], axis=1) for x in specs])
-        first = jnp.stack([jnp.concatenate([x[1][:, :INNER], x[0][:, :OUTER]], axis=1) for x in specs])
-        return swap(jnp.where(odd == 1, last, first), 1), swap(jnp.where(odd == 1, first, last), 0)
-
-    left_here, right_here, inner = lax.optimization_barrier((left, right, inner))
-    near_cross, near_inner = strips([left_here, specimen, right_here])
-    blocks, lines = near(place, probe, [left, specimen, right], col)
-    far0, far1, blocks, lines, near_inner = lax.optimization_barrier((far0, far1, blocks, lines, near_inner))
-    far_cross, far_inner = strips([(far0, far1)])
-    all_strips = (near_cross, near_inner, far_cross, far_inner)
-    wave, _, _, edge_strips = first_slice(place, probe, (cross, inner), all_strips, far0, (*bands0, col), blocks, lines)
-    specs = (left, specimen, right, far1)
-    return second_slice(place, wave, specs, edge_strips, (band1h, band1l, col), own)
+    per = probe.shape[3] // PIECES // LANES
+    far = PIECES - 1
+    near_task = (0, tuple(range(far)), tuple(range(1, far * per - 1)))
+    rest_tasks = (
+        (0, (far,), tuple(range(far * per - 1, PIECES * per + 1))),
+        (1, tuple(range(PIECES)), tuple(range(PIECES * per))),
+    )
+    blocks, lines = own_rows((near_task,), place, probe, [left, specimen, right], col)
+    far0, far1, blocks, lines = lax.optimization_barrier((far0, far1, blocks, lines))
+
+    def strips(specs, rows):
+        last = jnp.stack([x[:, own - rows :] for x in specs])
+        first = jnp.stack([x[:, :rows] for x in specs])
+        inner = swap(jnp.where(odd == 1, first, last), 0)
+        return swap(jnp.where(odd == 1, last, first), 1), inner
+
+    strips0 = strips([left[0], specimen[0], right[0], far0], OUTER)
+    strips1 = strips([left[1], specimen[1], right[1], far1], INNER)
+    _, lines, edge_rows = own_rows(rest_tasks, place, probe, [left, specimen, right, far0], col, (cross, inner), (blocks, lines))
+    wave = first_slice(place, edge_rows, strips0, (*bands0, col), lines)
+    return second_slice(place, wave, (left, specimen, right, far1), strips1, (band1h, band1l, col), own)
 
 
 def solution(mesh):

time: 60.7 us -> 52.7 us (0.87)
  the two profiles are of different devices: /device:TPU:71 before, /device:TPU:121 now
where the time goes in v1:
time: 52.7 us; the launch traced here: 52.5 us
  Pallas kernels  29.5 us (56%)
  starting transfers between devices  17.3 us (33%)
  waiting for transfers between devices  4.87 us (9%)
    ppermute x6, starting transfers between devices, swap(): return lax.ppermute(x, 'space', pairs + [(j, i) for i, j in pairs])  14.2 us
    pallas_call x2, Pallas kernels, own_rows(): pl.pallas_call(functools.partial(own_kernel, tasks, bool(halos)), out_sha...  8.58 us
    pallas_call x1, Pallas kernels, second_slice(): pl.pallas_call(second_kernel, out_shape=jax.ShapeDtypeStruct(shape, f32),...  6.83 us
    pallas_call x1, Pallas kernels, first_slice(): pl.pallas_call(first_kernel, out_shape=pltpu.VMEM((modes, bands[0].shape[...  6.5 us
    pallas_call x2, Pallas kernels, edges(): pl.pallas_call(functools.partial(edges_kernel, for_odd), out_shape=jax.Sh...  5.11 us
    ppermute x4, waiting for transfers between devices, turn(): return lax.ppermute(x, axis, [(i, (i + by) % n) for i in range(n)])  4.85 us
    ppermute x4, starting transfers between devices, turn(): return lax.ppermute(x, axis, [(i, (i + by) % n) for i in range(n)])  3.07 us
    pallas_call x1, Pallas kernels, prepare(): pl.pallas_call(prepare_kernel, out_shape=[pltpu.VMEM(s, bf16) for s in sh...  2.46 us
  transfers between devices with their start and end apart: 10, of which 2 were waited for; matrix products, arithmetic and copies ran while one was open for 1% of the time, Pallas kernels for 43%

profile of v1, /device:TPU:121, one launch (start us, length us, event | category | flops | bytes accessed | tf_op | source)
XLA Modules:
  0.0 52.5 jit_solution(701712467257940863)
XLA Ops:
  0.0 0.0 collective-permute-start
  0.0 1.5 %collective-permute-start.1 = (bf16[2,2,64,1024]{3,2,1,0:T(8,128)(2,1)}, bf16[2,2,64,1024]{3,2,1,0:T(8,128)(2,1)S(1)}, u32[]{:S(2)}, u32[]{:S(2)}) collective-permute-start(bf16[2,2,64,1024]{3,2,1,0:T(8,128)(2,1)} %own_spec.1), channel_id=1, source_target_pairs={{0,3},{1,0},{2,1},{3,2},{4,7},{5,4},{6,5},{7,6},{8,11},{9,8},{10,9... | collective-permute-start | bytes 1572872 | tf_op jit(solution)/shard_map/ppermute | solution.py:433
  1.5 0.1 pad_add_fusion.place
  1.5 2.7 %edges_cross.1 = f32[2,2,24,4096]{3,2,1,0:T(8,128)} custom-call(s32[4]{0:T(128)S(1)} %pad_add_fusion.place, f32[2,2,64,4096]{3,2,1,0:T(8,128)} %probe.7), custom_call_target="tpu_custom_call" | custom-call | tf_op jit(solution)/shard_map/edges_cross/pallas_call | solution.py:100
  4.3 0.0 copy-start.1
  4.3 0.0 copy-start
  4.3 4.4 %collective-permute-start.4 = (f32[2,2,24,4096]{3,2,1,0:T(8,128)}, f32[2,2,24,4096]{3,2,1,0:T(8,128)}, u32[]{:S(2)}, u32[]{:S(2)}) collective-permute-start(f32[2,2,24,4096]{3,2,1,0:T(8,128)} %edges_cross.1), channel_id=1, source_target_pairs={{4,8},{12,16},{20,24},{28,32},{36,40},{44,48},{52,56},{60,64},{68,... | collective-permute-start | bytes 4718600 | tf_op jit(solution)/shard_map/ppermute | solution.py:439
  8.7 2.4 %edges_inner.1 = f32[2,2,24,4096]{3,2,1,0:T(8,128)S(1)} custom-call(s32[4]{0:T(128)S(1)} %pad_add_fusion.place, f32[2,2,64,4096]{3,2,1,0:T(8,128)} %probe.7), custom_call_target="tpu_custom_call" | custom-call | tf_op jit(solution)/shard_map/edges_inner/pallas_call | solution.py:100
  11.1 0.5 collective-permute-start.5
  11.5 2.5 %prepare.1 = (bf16[192,224]{1,0:T(8,128)(2,1)S(1)}, bf16[192,224]{1,0:T(8,128)(2,1)S(1)}, bf16[128,192]{1,0:T(8,128)(2,1)S(1)}, bf16[128,192]{1,0:T(8,128)(2,1)S(1)}, bf16[1024,256]{1,0:T(8,128)(2,1)S(1)}) custom-call(f32[2,2,24]{2,1,0:T(2,128)S(1)} %copy-done.1), custom_call_target="tpu_custom_call" | custom-call | tf_op jit(solution)/shard_map/prepare/pallas_call | solution.py:137
  14.1 0.0 collective-permute-done.refs_0_.left
  14.1 0.0 collective-permute-done.1.refs_2_.right
  14.1 1.3 %collective-permute-start.2 = (bf16[2,64,1024]{2,1,0:T(8,128)(2,1)S(1)}, bf16[2,64,1024]{2,1,0:T(8,128)(2,1)S(1)}, u32[]{:S(2)}, u32[]{:S(2)}) collective-permute-start(bf16[2,64,1024]{2,1,0:T(8,128)(2,1)S(1)} %get-tuple-element.42), channel_id=1, source_target_pairs={{0,1},{1,2},{2,3},{3,0},{4,5},{5,6},{6,7},{7,4},{8,9},{9,10},{10,1... | collective-permute-start | bytes 786440 | tf_op jit(solution)/shard_map/ppermute | solution.py:433
  15.5 0.3 collective-permute-start.3
  15.8 3.2 %own_near.1 = (bf16[2,2048,512]{2,1,0:T(8,128)(2,1)S(1)}, bf16[2,2,128,4096]{3,2,1,0:T(8,128)(2,1)S(1)}) custom-call(s32[4]{0:T(128)S(1)} %pad_add_fusion.place, f32[2,2,64,4096]{3,2,1,0:T(8,128)} %probe.7, bf16[2,2,64,1024]{3,2,1,0:T(8,128)(2,1)S(1)} %collective-permute-done.refs_0_.left, bf16[2,2,64,1024]{3,2,1,0:T(8,128)(2,1)S(1)} %copy-done, ...), custom_call_target="tpu_custom_call" | custom-call | flops 4000000000 | bytes 10000000 | tf_op jit(solution)/shard_map/own_near/pallas_call | solution.py:301
  19.1 1.5 %collective-permute-done.2.refs_3_ = bf16[2,64,1024]{2,1,0:T(8,128)(2,1)S(1)} collective-permute-done((bf16[2,64,1024]{2,1,0:T(8,128)(2,1)S(1)}, bf16[2,64,1024]{2,1,0:T(8,128)(2,1)S(1)}, u32[]{:S(2)}, u32[]{:S(2)}) %collective-permute-start.2) | collective-permute-done | bytes 262176 | tf_op jit(solution)/shard_map/ppermute | solution.py:433
  20.6 3.3 %collective-permute-done.3.far_spec = bf16[2,64,1024]{2,1,0:T(8,128)(2,1)S(1)} collective-permute-done((bf16[2,64,1024]{2,1,0:T(8,128)(2,1)S(1)}, bf16[2,64,1024]{2,1,0:T(8,128)(2,1)S(1)}, u32[]{:S(2)}, u32[]{:S(2)}) %collective-permute-start.3) | collective-permute-done | bytes 262176 | tf_op jit(solution)/shard_map/ppermute | solution.py:433
  23.9 0.1 broadcast_select_fusion
  24.1 4.2 %collective-permute-start.6 = (bf16[4,2,24,1024]{3,2,1,0:T(8,128)(2,1)S(1)}, bf16[4,2,24,1024]{3,2,1,0:T(8,128)(2,1)S(1)}, u32[]{:S(2)}, u32[]{:S(2)}) collective-permute-start(bf16[4,2,24,1024]{3,2,1,0:T(8,128)(2,1)S(1)} %get-tuple-element.38), channel_id=1, source_target_pairs={{4,8},{12,16},{20,24},{28,32},{36,40},{44,48},{52,56},{60,64},{68,... | collective-permute-start | bytes 1179656 | tf_op jit(solution)/shard_map/ppermute | solution.py:439
  28.2 0.1 collective-permute-start.7
  28.3 0.1 broadcast_select_fusion.2
  28.4 3.2 %collective-permute-start.8 = (bf16[4,2,16,1024]{3,2,1,0:T(8,128)(2,1)S(1)}, bf16[4,2,16,1024]{3,2,1,0:T(8,128)(2,1)S(1)}, u32[]{:S(2)}, u32[]{:S(2)}) collective-permute-start(bf16[4,2,16,1024]{3,2,1,0:T(8,128)(2,1)S(1)} %get-tuple-element.40), channel_id=1, source_target_pairs={{4,8},{12,16},{20,24},{28,32},{36,40},{44,48},{52,56},{60,64},{68,... | collective-permute-start | bytes 786440 | tf_op jit(solution)/shard_map/ppermute | solution.py:439
  31.6 0.0 collective-permute-done.4.refs_5_
  31.6 2.0 %collective-permute-start.9 = (bf16[4,2,16,1024]{3,2,1,0:T(8,128)(2,1)S(1)}, bf16[4,2,16,1024]{3,2,1,0:T(8,128)(2,1)S(1)}, u32[]{:S(2)}, u32[]{:S(2)}) collective-permute-start(bf16[4,2,16,1024]{3,2,1,0:T(8,128)(2,1)S(1)} %get-tuple-element.39), channel_id=1, source_target_pairs={{0,4},{8,12},{16,20},{24,28},{32,36},{40,44},{48,52},{56,60},{64,6... | collective-permute-start | bytes 786440 | tf_op jit(solution)/shard_map/ppermute | solution.py:439
  33.6 0.0 collective-permute-done.5.refs_6_
  33.6 5.4 %own_rest.1 = (bf16[2,2048,512]{2,1,0:T(8,128)(2,1)S(1)}, bf16[2,2,128,4096]{3,2,1,0:T(8,128)(2,1)S(1)}, f32[2,2,4,2,24,1024]{5,4,3,2,1,0:T(8,128)S(1)}) custom-call(s32[4]{0:T(128)S(1)} %pad_add_fusion.place, f32[2,2,64,4096]{3,2,1,0:T(8,128)} %probe.7, ...), custom_call_target="tpu_custom_call", output_to_operand_aliasing={{0}: (9, {}), {1}: (10, {})} | custom-call | flops 4000000000 | bytes 10000000 | tf_op jit(solution)/shard_map/own_rest/pallas_call | solution.py:301
  39.0 0.0 collective-permute-done.6.strips_cross
  39.0 0.0 collective-permute-done.7.strips_inner
  39.0 6.5 %first_slice.1.wave = f32[2,192,4096]{2,1,0:T(8,128)S(1)} custom-call(s32[4]{0:T(128)S(1)} %pad_add_fusion.place, f32[2,2,4,2,24,1024]{5,4,3,2,1,0:T(8,128)S(1)} %get-tuple-element.30.edge_rows, bf16[4,2,24,1024]{3,2,1,0:T(8,128)(2,1)S(1)} %collective-permute-done.6.strips_cross, bf16[4,2,24,1024]{3,2,1,0:T(8,128)(2,1)S(1)} %collective-permute-done.7.strips_inner, ...), custom_call_target="tpu_custom_call" | custom-call | tf_op jit(solution)/shard_map/first_slice/pallas_call | solution.py:348
  45.5 0.0 collective-permute-done.8.strips_cross
  45.5 0.0 collective-permute-done.9.strips_inner
  45.5 6.8 %second_slice.1 = f32[2,2,64,4096]{3,2,1,0:T(8,128)} custom-call(s32[4]{0:T(128)S(1)} %pad_add_fusion.place, f32[2,192,4096]{2,1,0:T(8,128)S(1)} %first_slice.1.wave, bf16[2,2,64,1024]{3,2,1,0:T(8,128)(2,1)S(1)} %collective-permute-done.refs_0_.left, bf16[2,2,64,1024]{3,2,1,0:T(8,128)(2,1)S(1)} %copy-done, ...), custom_call_target="tpu_custom_call" | custom-call | tf_op jit(solution)/shard_map/second_slice/pallas_call | solution.py:413
  (11 shorter events, 0.2 us)
Async XLA Ops:
  0.0 14.1 %collective-permute-start = (bf16[2,2,64,1024]{3,2,1,0:T(8,128)(2,1)}, bf16[2,2,64,1024]{3,2,1,0:T(8,128)(2,1)S(1)}, u32[]{:S(2)}, u32[]{:S(2)}) collective-permute-start(bf16[2,2,64,1024]{3,2,1,0:T(8,128)(2,1)} %own_spec.1), channel_id=1, source_target_pairs={{0,1},{1,2},{2,3},{3,0},{4,5},{5,6},{6,7},{7,4},{8,9},{9,10},{10,1... | collective-permute-start | bytes 1572872 | tf_op jit(solution)/shard_map/ppermute | solution.py:433
  0.0 14.1 %collective-permute-start.1 = (bf16[2,2,64,1024]{3,2,1,0:T(8,128)(2,1)}, bf16[2,2,64,1024]{3,2,1,0:T(8,128)(2,1)S(1)}, u32[]{:S(2)}, u32[]{:S(2)}) collective-permute-start(bf16[2,2,64,1024]{3,2,1,0:T(8,128)(2,1)} %own_spec.1), channel_id=1, source_target_pairs={{0,3},{1,0},{2,1},{3,2},{4,7},{5,4},{6,5},{7,6},{8,11},{9,8},{10,9... | collective-permute-start | bytes 1572872 | tf_op jit(solution)/shard_map/ppermute | solution.py:433
  4.3 7.2 %copy-start.1 = (f32[2,2,24]{2,1,0:T(2,128)S(1)}, f32[2,2,24]{2,1,0:T(2,128)}, u32[]{:S(2)}) copy-start(f32[2,2,24]{2,1,0:T(2,128)} %kernels.1) | copy-start | bytes 1156
  4.3 9.7 %copy-start = (bf16[2,2,64,1024]{3,2,1,0:T(8,128)(2,1)S(1)}, bf16[2,2,64,1024]{3,2,1,0:T(8,128)(2,1)}, u32[]{:S(2)}) copy-start(bf16[2,2,64,1024]{3,2,1,0:T(8,128)(2,1)} %own_spec.1) | copy-start | bytes 1572868
  4.3 27.3 %collective-permute-start.4 = (f32[2,2,24,4096]{3,2,1,0:T(8,128)}, f32[2,2,24,4096]{3,2,1,0:T(8,128)}, u32[]{:S(2)}, u32[]{:S(2)}) collective-permute-start(f32[2,2,24,4096]{3,2,1,0:T(8,128)} %edges_cross.1), channel_id=1, source_target_pairs={{4,8},{12,16},{20,24},{28,32},{36,40},{44,48},{52,56},{60,64},{68,... | collective-permute-start | bytes 4718600 | tf_op jit(solution)/shard_map/ppermute | solution.py:439
  11.1 22.5 %collective-permute-start.5 = (f32[2,2,24,4096]{3,2,1,0:T(8,128)S(1)}, f32[2,2,24,4096]{3,2,1,0:T(8,128)}, u32[]{:S(2)}, u32[]{:S(2)}) collective-permute-start(f32[2,2,24,4096]{3,2,1,0:T(8,128)S(1)} %edges_inner.1), channel_id=1, source_target_pairs={{0,4},{8,12},{16,20},{24,28},{32,36},{40,44},{48,52},{56,60},{64,6... | collective-permute-start | bytes 4718600 | tf_op jit(solution)/shard_map/ppermute | solution.py:439
  14.1 6.5 %collective-permute-start.2 = (bf16[2,64,1024]{2,1,0:T(8,128)(2,1)S(1)}, bf16[2,64,1024]{2,1,0:T(8,128)(2,1)S(1)}, u32[]{:S(2)}, u32[]{:S(2)}) collective-permute-start(bf16[2,64,1024]{2,1,0:T(8,128)(2,1)S(1)} %get-tuple-element.42), channel_id=1, source_target_pairs={{0,1},{1,2},{2,3},{3,0},{4,5},{5,6},{6,7},{7,4},{8,9},{9,10},{10,1... | collective-permute-start | bytes 786440 | tf_op jit(solution)/shard_map/ppermute | solution.py:433
  15.5 8.4 %collective-permute-start.3 = (bf16[2,64,1024]{2,1,0:T(8,128)(2,1)S(1)}, bf16[2,64,1024]{2,1,0:T(8,128)(2,1)S(1)}, u32[]{:S(2)}, u32[]{:S(2)}) collective-permute-start(bf16[2,64,1024]{2,1,0:T(8,128)(2,1)S(1)} %get-tuple-element.46), channel_id=1, source_target_pairs={{0,3},{1,0},{2,1},{3,2},{4,7},{5,4},{6,5},{7,6},{8,11},{9,8},{10,9... | collective-permute-start | bytes 786440 | tf_op jit(solution)/shard_map/ppermute | solution.py:433
  24.1 14.9 %collective-permute-start.6 = (bf16[4,2,24,1024]{3,2,1,0:T(8,128)(2,1)S(1)}, bf16[4,2,24,1024]{3,2,1,0:T(8,128)(2,1)S(1)}, u32[]{:S(2)}, u32[]{:S(2)}) collective-permute-start(bf16[4,2,24,1024]{3,2,1,0:T(8,128)(2,1)S(1)} %get-tuple-element.38), channel_id=1, source_target_pairs={{4,8},{12,16},{20,24},{28,32},{36,40},{44,48},{52,56},{60,64},{68,... | collective-permute-start | bytes 1179656 | tf_op jit(solution)/shard_map/ppermute | solution.py:439
  28.2 10.8 %collective-permute-start.7 = (bf16[4,2,24,1024]{3,2,1,0:T(8,128)(2,1)S(1)}, bf16[4,2,24,1024]{3,2,1,0:T(8,128)(2,1)S(1)}, u32[]{:S(2)}, u32[]{:S(2)}) collective-permute-start(bf16[4,2,24,1024]{3,2,1,0:T(8,128)(2,1)S(1)} %get-tuple-element.37), channel_id=1, source_target_pairs={{0,4},{8,12},{16,20},{24,28},{32,36},{40,44},{48,52},{56,60},{64,6... | collective-permute-start | bytes 1179656 | tf_op jit(solution)/shard_map/ppermute | solution.py:439
  28.4 17.1 %collective-permute-start.8 = (bf16[4,2,16,1024]{3,2,1,0:T(8,128)(2,1)S(1)}, bf16[4,2,16,1024]{3,2,1,0:T(8,128)(2,1)S(1)}, u32[]{:S(2)}, u32[]{:S(2)}) collective-permute-start(bf16[4,2,16,1024]{3,2,1,0:T(8,128)(2,1)S(1)} %get-tuple-element.40), channel_id=1, source_target_pairs={{4,8},{12,16},{20,24},{28,32},{36,40},{44,48},{52,56},{60,64},{68,... | collective-permute-start | bytes 786440 | tf_op jit(solution)/shard_map/ppermute | solution.py:439
  31.6 13.9 %collective-permute-start.9 = (bf16[4,2,16,1024]{3,2,1,0:T(8,128)(2,1)S(1)}, bf16[4,2,16,1024]{3,2,1,0:T(8,128)(2,1)S(1)}, u32[]{:S(2)}, u32[]{:S(2)}) collective-permute-start(bf16[4,2,16,1024]{3,2,1,0:T(8,128)(2,1)S(1)} %get-tuple-element.39), channel_id=1, source_target_pairs={{0,4},{8,12},{16,20},{24,28},{32,36},{40,44},{48,52},{56,60},{64,6... | collective-permute-start | bytes 786440 | tf_op jit(solution)/shard_map/ppermute | solution.py:439

commit v2 on v1

--- a/solution.py
+++ b/solution.py
@@ -333,7 +333,9 @@
                     for e in range(2)
                 ]
                 put(outer.at[m], (q * piece + at.start) // LANES, [jnp.concatenate([planes[0][p], planes[1][p]], axis=0) for p in range(2)])
+    for m in range(modes):
         column_stage(place, outer.at[m], outer_tails.at[m], col, list(range(width // LANES)), edge, keep_columns(outer_lines.at[m], edge))
+    for m in range(modes):
         for at in chunks(width):
             x = [jnp.concatenate([lines[m, k, :, at], outer_lines[m, k, :, at]], axis=0) for k in range(2)]
             wave[m, :, at] = row_stage(*x, high, low)
@@ -393,6 +395,8 @@
                 result = row_stage(*split(jnp.concatenate([*inside, *outside], axis=0)), high, low)
                 put(blocks.at[m], cells.start // LANES, (result[:rows], result[rows:]))
 
+    for m in range(modes):
+
         def emit(j, real, imag, m=m):
             stage[m, 0, :, lanes(j)] = real
             stage[m, 1, :, lanes(j)] = imag

time: 52.7 us -> 53.2 us (level)
  no operation moved by 1% of the time
where the time goes in v2:
time: 53.2 us; the launch traced here: 53 us
  Pallas kernels  29.9 us (56%)
  starting transfers between devices  17.3 us (33%)
  waiting for transfers between devices  4.87 us (9%)
    ppermute x6, starting transfers between devices, swap(): return lax.ppermute(x, 'space', pairs + [(j, i) for i, j in pairs])  14.2 us
    pallas_call x2, Pallas kernels, own_rows(): pl.pallas_call(functools.partial(own_kernel, tasks, bool(halos)), out_sha...  8.58 us
    pallas_call x1, Pallas kernels, second_slice(): pl.pallas_call(second_kernel, out_shape=jax.ShapeDtypeStruct(shape, f32),...  7.16 us
    pallas_call x1, Pallas kernels, first_slice(): pl.pallas_call(first_kernel, out_shape=pltpu.VMEM((modes, bands[0].shape[...  6.6 us
    pallas_call x2, Pallas kernels, edges(): pl.pallas_call(functools.partial(edges_kernel, for_odd), out_shape=jax.Sh...  5.11 us
    ppermute x4, waiting for transfers between devices, turn(): return lax.ppermute(x, axis, [(i, (i + by) % n) for i in range(n)])  4.85 us
    ppermute x4, starting transfers between devices, turn(): return lax.ppermute(x, axis, [(i, (i + by) % n) for i in range(n)])  3.07 us
    pallas_call x1, Pallas kernels, prepare(): pl.pallas_call(prepare_kernel, out_shape=[pltpu.VMEM(s, bf16) for s in sh...  2.46 us
  transfers between devices with their start and end apart: 10, of which 2 were waited for; matrix products, arithmetic and copies ran while one was open for 1% of the time, Pallas kernels for 43%

profile of v2, /device:TPU:121, one launch (start us, length us, event | category | flops | bytes accessed | tf_op | source)
XLA Modules:
  0.0 53.0 jit_solution(6532955504716088281)
XLA Ops:
  0.0 0.0 collective-permute-start
  0.0 1.5 %collective-permute-start.1 = (bf16[2,2,64,1024]{3,2,1,0:T(8,128)(2,1)}, bf16[2,2,64,1024]{3,2,1,0:T(8,128)(2,1)S(1)}, u32[]{:S(2)}, u32[]{:S(2)}) collective-permute-start(bf16[2,2,64,1024]{3,2,1,0:T(8,128)(2,1)} %own_spec.1), channel_id=1, source_target_pairs={{0,3},{1,0},{2,1},{3,2},{4,7},{5,4},{6,5},{7,6},{8,11},{9,8},{10,9... | collective-permute-start | bytes 1572872 | tf_op jit(solution)/shard_map/ppermute | solution.py:437
  1.5 0.1 pad_add_fusion.place
  1.5 2.7 %edges_cross.1 = f32[2,2,24,4096]{3,2,1,0:T(8,128)} custom-call(s32[4]{0:T(128)S(1)} %pad_add_fusion.place, f32[2,2,64,4096]{3,2,1,0:T(8,128)} %probe.7), custom_call_target="tpu_custom_call" | custom-call | tf_op jit(solution)/shard_map/edges_cross/pallas_call | solution.py:100
  4.3 0.0 copy-start.1
  4.3 0.0 copy-start
  4.3 4.4 %collective-permute-start.4 = (f32[2,2,24,4096]{3,2,1,0:T(8,128)}, f32[2,2,24,4096]{3,2,1,0:T(8,128)}, u32[]{:S(2)}, u32[]{:S(2)}) collective-permute-start(f32[2,2,24,4096]{3,2,1,0:T(8,128)} %edges_cross.1), channel_id=1, source_target_pairs={{4,8},{12,16},{20,24},{28,32},{36,40},{44,48},{52,56},{60,64},{68,... | collective-permute-start | bytes 4718600 | tf_op jit(solution)/shard_map/ppermute | solution.py:443
  8.7 2.4 %edges_inner.1 = f32[2,2,24,4096]{3,2,1,0:T(8,128)S(1)} custom-call(s32[4]{0:T(128)S(1)} %pad_add_fusion.place, f32[2,2,64,4096]{3,2,1,0:T(8,128)} %probe.7), custom_call_target="tpu_custom_call" | custom-call | tf_op jit(solution)/shard_map/edges_inner/pallas_call | solution.py:100
  11.1 0.5 collective-permute-start.5
  11.5 2.5 %prepare.1 = (bf16[192,224]{1,0:T(8,128)(2,1)S(1)}, bf16[192,224]{1,0:T(8,128)(2,1)S(1)}, bf16[128,192]{1,0:T(8,128)(2,1)S(1)}, bf16[128,192]{1,0:T(8,128)(2,1)S(1)}, bf16[1024,256]{1,0:T(8,128)(2,1)S(1)}) custom-call(f32[2,2,24]{2,1,0:T(2,128)S(1)} %copy-done.1), custom_call_target="tpu_custom_call" | custom-call | tf_op jit(solution)/shard_map/prepare/pallas_call | solution.py:137
  14.1 0.0 collective-permute-done.refs_0_.left
  14.1 0.0 collective-permute-done.1.refs_2_.right
  14.1 1.3 %collective-permute-start.2 = (bf16[2,64,1024]{2,1,0:T(8,128)(2,1)S(1)}, bf16[2,64,1024]{2,1,0:T(8,128)(2,1)S(1)}, u32[]{:S(2)}, u32[]{:S(2)}) collective-permute-start(bf16[2,64,1024]{2,1,0:T(8,128)(2,1)S(1)} %get-tuple-element.42), channel_id=1, source_target_pairs={{0,1},{1,2},{2,3},{3,0},{4,5},{5,6},{6,7},{7,4},{8,9},{9,10},{10,1... | collective-permute-start | bytes 786440 | tf_op jit(solution)/shard_map/ppermute | solution.py:437
  15.5 0.3 collective-permute-start.3
  15.8 3.2 %own_near.1 = (bf16[2,2048,512]{2,1,0:T(8,128)(2,1)S(1)}, bf16[2,2,128,4096]{3,2,1,0:T(8,128)(2,1)S(1)}) custom-call(s32[4]{0:T(128)S(1)} %pad_add_fusion.place, f32[2,2,64,4096]{3,2,1,0:T(8,128)} %probe.7, bf16[2,2,64,1024]{3,2,1,0:T(8,128)(2,1)S(1)} %collective-permute-done.refs_0_.left, bf16[2,2,64,1024]{3,2,1,0:T(8,128)(2,1)S(1)} %copy-done, ...), custom_call_target="tpu_custom_call" | custom-call | flops 4000000000 | bytes 10000000 | tf_op jit(solution)/shard_map/own_near/pallas_call | solution.py:301
  19.1 1.5 %collective-permute-done.2.refs_3_ = bf16[2,64,1024]{2,1,0:T(8,128)(2,1)S(1)} collective-permute-done((bf16[2,64,1024]{2,1,0:T(8,128)(2,1)S(1)}, bf16[2,64,1024]{2,1,0:T(8,128)(2,1)S(1)}, u32[]{:S(2)}, u32[]{:S(2)}) %collective-permute-start.2) | collective-permute-done | bytes 262176 | tf_op jit(solution)/shard_map/ppermute | solution.py:437
  20.6 3.3 %collective-permute-done.3.far_spec = bf16[2,64,1024]{2,1,0:T(8,128)(2,1)S(1)} collective-permute-done((bf16[2,64,1024]{2,1,0:T(8,128)(2,1)S(1)}, bf16[2,64,1024]{2,1,0:T(8,128)(2,1)S(1)}, u32[]{:S(2)}, u32[]{:S(2)}) %collective-permute-start.3) | collective-permute-done | bytes 262176 | tf_op jit(solution)/shard_map/ppermute | solution.py:437
  23.9 0.1 broadcast_select_fusion
  24.1 4.2 %collective-permute-start.6 = (bf16[4,2,24,1024]{3,2,1,0:T(8,128)(2,1)S(1)}, bf16[4,2,24,1024]{3,2,1,0:T(8,128)(2,1)S(1)}, u32[]{:S(2)}, u32[]{:S(2)}) collective-permute-start(bf16[4,2,24,1024]{3,2,1,0:T(8,128)(2,1)S(1)} %get-tuple-element.38), channel_id=1, source_target_pairs={{4,8},{12,16},{20,24},{28,32},{36,40},{44,48},{52,56},{60,64},{68,... | collective-permute-start | bytes 1179656 | tf_op jit(solution)/shard_map/ppermute | solution.py:443
  28.2 0.1 collective-permute-start.7
  28.3 0.1 broadcast_select_fusion.2
  28.4 3.2 %collective-permute-start.8 = (bf16[4,2,16,1024]{3,2,1,0:T(8,128)(2,1)S(1)}, bf16[4,2,16,1024]{3,2,1,0:T(8,128)(2,1)S(1)}, u32[]{:S(2)}, u32[]{:S(2)}) collective-permute-start(bf16[4,2,16,1024]{3,2,1,0:T(8,128)(2,1)S(1)} %get-tuple-element.40), channel_id=1, source_target_pairs={{4,8},{12,16},{20,24},{28,32},{36,40},{44,48},{52,56},{60,64},{68,... | collective-permute-start | bytes 786440 | tf_op jit(solution)/shard_map/ppermute | solution.py:443
  31.6 0.0 collective-permute-done.4.refs_5_
  31.6 2.0 %collective-permute-start.9 = (bf16[4,2,16,1024]{3,2,1,0:T(8,128)(2,1)S(1)}, bf16[4,2,16,1024]{3,2,1,0:T(8,128)(2,1)S(1)}, u32[]{:S(2)}, u32[]{:S(2)}) collective-permute-start(bf16[4,2,16,1024]{3,2,1,0:T(8,128)(2,1)S(1)} %get-tuple-element.39), channel_id=1, source_target_pairs={{0,4},{8,12},{16,20},{24,28},{32,36},{40,44},{48,52},{56,60},{64,6... | collective-permute-start | bytes 786440 | tf_op jit(solution)/shard_map/ppermute | solution.py:443
  33.6 0.0 collective-permute-done.5.refs_6_
  33.6 5.4 %own_rest.1 = (bf16[2,2048,512]{2,1,0:T(8,128)(2,1)S(1)}, bf16[2,2,128,4096]{3,2,1,0:T(8,128)(2,1)S(1)}, f32[2,2,4,2,24,1024]{5,4,3,2,1,0:T(8,128)S(1)}) custom-call(s32[4]{0:T(128)S(1)} %pad_add_fusion.place, f32[2,2,64,4096]{3,2,1,0:T(8,128)} %probe.7, ...), custom_call_target="tpu_custom_call", output_to_operand_aliasing={{0}: (9, {}), {1}: (10, {})} | custom-call | flops 4000000000 | bytes 10000000 | tf_op jit(solution)/shard_map/own_rest/pallas_call | solution.py:301
  39.0 0.0 collective-permute-done.6.strips_cross
  39.0 0.0 collective-permute-done.7.strips_inner
  39.0 6.6 %first_slice.1.wave = f32[2,192,4096]{2,1,0:T(8,128)S(1)} custom-call(s32[4]{0:T(128)S(1)} %pad_add_fusion.place, f32[2,2,4,2,24,1024]{5,4,3,2,1,0:T(8,128)S(1)} %get-tuple-element.30.edge_rows, bf16[4,2,24,1024]{3,2,1,0:T(8,128)(2,1)S(1)} %collective-permute-done.6.strips_cross, bf16[4,2,24,1024]{3,2,1,0:T(8,128)(2,1)S(1)} %collective-permute-done.7.strips_inner, ...), custom_call_target="tpu_custom_call" | custom-call | tf_op jit(solution)/shard_map/first_slice/pallas_call | solution.py:350
  45.6 0.0 collective-permute-done.8.strips_cross
  45.6 0.0 collective-permute-done.9.strips_inner
  45.6 7.2 %second_slice.1 = f32[2,2,64,4096]{3,2,1,0:T(8,128)} custom-call(s32[4]{0:T(128)S(1)} %pad_add_fusion.place, f32[2,192,4096]{2,1,0:T(8,128)S(1)} %first_slice.1.wave, bf16[2,2,64,1024]{3,2,1,0:T(8,128)(2,1)S(1)} %collective-permute-done.refs_0_.left, bf16[2,2,64,1024]{3,2,1,0:T(8,128)(2,1)S(1)} %copy-done, ...), custom_call_target="tpu_custom_call" | custom-call | tf_op jit(solution)/shard_map/second_slice/pallas_call | solution.py:417
  (11 shorter events, 0.2 us)
Async XLA Ops:
  0.0 14.1 %collective-permute-start = (bf16[2,2,64,1024]{3,2,1,0:T(8,128)(2,1)}, bf16[2,2,64,1024]{3,2,1,0:T(8,128)(2,1)S(1)}, u32[]{:S(2)}, u32[]{:S(2)}) collective-permute-start(bf16[2,2,64,1024]{3,2,1,0:T(8,128)(2,1)} %own_spec.1), channel_id=1, source_target_pairs={{0,1},{1,2},{2,3},{3,0},{4,5},{5,6},{6,7},{7,4},{8,9},{9,10},{10,1... | collective-permute-start | bytes 1572872 | tf_op jit(solution)/shard_map/ppermute | solution.py:437
  0.0 14.1 %collective-permute-start.1 = (bf16[2,2,64,1024]{3,2,1,0:T(8,128)(2,1)}, bf16[2,2,64,1024]{3,2,1,0:T(8,128)(2,1)S(1)}, u32[]{:S(2)}, u32[]{:S(2)}) collective-permute-start(bf16[2,2,64,1024]{3,2,1,0:T(8,128)(2,1)} %own_spec.1), channel_id=1, source_target_pairs={{0,3},{1,0},{2,1},{3,2},{4,7},{5,4},{6,5},{7,6},{8,11},{9,8},{10,9... | collective-permute-start | bytes 1572872 | tf_op jit(solution)/shard_map/ppermute | solution.py:437
  4.3 7.2 %copy-start.1 = (f32[2,2,24]{2,1,0:T(2,128)S(1)}, f32[2,2,24]{2,1,0:T(2,128)}, u32[]{:S(2)}) copy-start(f32[2,2,24]{2,1,0:T(2,128)} %kernels.1) | copy-start | bytes 1156
  4.3 9.7 %copy-start = (bf16[2,2,64,1024]{3,2,1,0:T(8,128)(2,1)S(1)}, bf16[2,2,64,1024]{3,2,1,0:T(8,128)(2,1)}, u32[]{:S(2)}) copy-start(bf16[2,2,64,1024]{3,2,1,0:T(8,128)(2,1)} %own_spec.1) | copy-start | bytes 1572868
  4.3 27.3 %collective-permute-start.4 = (f32[2,2,24,4096]{3,2,1,0:T(8,128)}, f32[2,2,24,4096]{3,2,1,0:T(8,128)}, u32[]{:S(2)}, u32[]{:S(2)}) collective-permute-start(f32[2,2,24,4096]{3,2,1,0:T(8,128)} %edges_cross.1), channel_id=1, source_target_pairs={{4,8},{12,16},{20,24},{28,32},{36,40},{44,48},{52,56},{60,64},{68,... | collective-permute-start | bytes 4718600 | tf_op jit(solution)/shard_map/ppermute | solution.py:443
  11.1 22.5 %collective-permute-start.5 = (f32[2,2,24,4096]{3,2,1,0:T(8,128)S(1)}, f32[2,2,24,4096]{3,2,1,0:T(8,128)}, u32[]{:S(2)}, u32[]{:S(2)}) collective-permute-start(f32[2,2,24,4096]{3,2,1,0:T(8,128)S(1)} %edges_inner.1), channel_id=1, source_target_pairs={{0,4},{8,12},{16,20},{24,28},{32,36},{40,44},{48,52},{56,60},{64,6... | collective-permute-start | bytes 4718600 | tf_op jit(solution)/shard_map/ppermute | solution.py:443
  14.1 6.5 %collective-permute-start.2 = (bf16[2,64,1024]{2,1,0:T(8,128)(2,1)S(1)}, bf16[2,64,1024]{2,1,0:T(8,128)(2,1)S(1)}, u32[]{:S(2)}, u32[]{:S(2)}) collective-permute-start(bf16[2,64,1024]{2,1,0:T(8,128)(2,1)S(1)} %get-tuple-element.42), channel_id=1, source_target_pairs={{0,1},{1,2},{2,3},{3,0},{4,5},{5,6},{6,7},{7,4},{8,9},{9,10},{10,1... | collective-permute-start | bytes 786440 | tf_op jit(solution)/shard_map/ppermute | solution.py:437
  15.5 8.4 %collective-permute-start.3 = (bf16[2,64,1024]{2,1,0:T(8,128)(2,1)S(1)}, bf16[2,64,1024]{2,1,0:T(8,128)(2,1)S(1)}, u32[]{:S(2)}, u32[]{:S(2)}) collective-permute-start(bf16[2,64,1024]{2,1,0:T(8,128)(2,1)S(1)} %get-tuple-element.46), channel_id=1, source_target_pairs={{0,3},{1,0},{2,1},{3,2},{4,7},{5,4},{6,5},{7,6},{8,11},{9,8},{10,9... | collective-permute-start | bytes 786440 | tf_op jit(solution)/shard_map/ppermute | solution.py:437
  24.1 14.9 %collective-permute-start.6 = (bf16[4,2,24,1024]{3,2,1,0:T(8,128)(2,1)S(1)}, bf16[4,2,24,1024]{3,2,1,0:T(8,128)(2,1)S(1)}, u32[]{:S(2)}, u32[]{:S(2)}) collective-permute-start(bf16[4,2,24,1024]{3,2,1,0:T(8,128)(2,1)S(1)} %get-tuple-element.38), channel_id=1, source_target_pairs={{4,8},{12,16},{20,24},{28,32},{36,40},{44,48},{52,56},{60,64},{68,... | collective-permute-start | bytes 1179656 | tf_op jit(solution)/shard_map/ppermute | solution.py:443
  28.2 10.8 %collective-permute-start.7 = (bf16[4,2,24,1024]{3,2,1,0:T(8,128)(2,1)S(1)}, bf16[4,2,24,1024]{3,2,1,0:T(8,128)(2,1)S(1)}, u32[]{:S(2)}, u32[]{:S(2)}) collective-permute-start(bf16[4,2,24,1024]{3,2,1,0:T(8,128)(2,1)S(1)} %get-tuple-element.37), channel_id=1, source_target_pairs={{0,4},{8,12},{16,20},{24,28},{32,36},{40,44},{48,52},{56,60},{64,6... | collective-permute-start | bytes 1179656 | tf_op jit(solution)/shard_map/ppermute | solution.py:443
  28.4 17.2 %collective-permute-start.8 = (bf16[4,2,16,1024]{3,2,1,0:T(8,128)(2,1)S(1)}, bf16[4,2,16,1024]{3,2,1,0:T(8,128)(2,1)S(1)}, u32[]{:S(2)}, u32[]{:S(2)}) collective-permute-start(bf16[4,2,16,1024]{3,2,1,0:T(8,128)(2,1)S(1)} %get-tuple-element.40), channel_id=1, source_target_pairs={{4,8},{12,16},{20,24},{28,32},{36,40},{44,48},{52,56},{60,64},{68,... | collective-permute-start | bytes 786440 | tf_op jit(solution)/shard_map/ppermute | solution.py:443
  31.6 14.0 %collective-permute-start.9 = (bf16[4,2,16,1024]{3,2,1,0:T(8,128)(2,1)S(1)}, bf16[4,2,16,1024]{3,2,1,0:T(8,128)(2,1)S(1)}, u32[]{:S(2)}, u32[]{:S(2)}) collective-permute-start(bf16[4,2,16,1024]{3,2,1,0:T(8,128)(2,1)S(1)} %get-tuple-element.39), channel_id=1, source_target_pairs={{0,4},{8,12},{16,20},{24,28},{32,36},{40,44},{48,52},{56,60},{64,6... | collective-permute-start | bytes 786440 | tf_op jit(solution)/shard_map/ppermute | solution.py:443
